TPU v7x, 256 devices: a whole 4x4x8 slice. The times are simulated.
256 devices in a mesh: row: 32 (over y, z), col: 8 (over x, core).
Axes of the slice: x: 4, y: 4, z: 8, core: 2. Of those that a mesh axis runs over, the one named last changes fastest.
Arguments:
- features: bfloat16 [65536, 128], P(('row', 'col')), may hold values from -6 to 6
- tiles: bfloat16 [32, 8, 128, 128, 128], P('row', 'col'), may hold values from -6 to 6
- block_rows: int32 [32, 8, 128], P('row', 'col'), may hold values from 0 to 15
- block_cols: int32 [32, 8, 128], P('row', 'col'), may hold values from 0 to 63
- labels: int32 [65536], P(('row', 'col')), may hold values from 0 to 171
- train_mask: int32 [65536], P(('row', 'col')), may hold values 0 or 1
- self_first: bfloat16 [128, 256], replicated, may hold values from -0.5 to 0.5
- neigh_first: bfloat16 [128, 256], replicated, may hold values from -0.5 to 0.5
- bias_first: float32 [256], replicated, may hold values from -4 to 4
- self_second: bfloat16 [256, 172], replicated, may hold values from -0.375 to 0.375
- neigh_second: bfloat16 [256, 172], replicated, may hold values from -0.375 to 0.375
- bias_second: float32 [172], replicated, may hold values from -4 to 4
Outputs:
- grad_self_first: float32 [128, 256], replicated
- grad_neigh_first: float32 [128, 256], replicated
- grad_bias_first: float32 [256], replicated
- grad_self_second: float32 [256, 172], replicated
- grad_neigh_second: float32 [256, 172], replicated
- grad_bias_second: float32 [172], replicated
All inputs are finite; a program needn't handle non-finite values. No bound on the sum of `train_mask` on one device may be relied on, other than what follows from the above.
Results may differ from a plain program's by a relative error of at most 0.014.
The roundings to bfloat16 on the way count: a program that leaves them out, or rounds other values in their place, can miss the bound.
Values may be sent and summed in bfloat16 or wider, within the bound.
No kernel may reach another device: no remote copies, remote signals or barrier semaphores. Data moves between devices by JAX's collectives and lax.ppermute only.
A program may use at most 128 MiB of HBM per device.

v0:
```python
import functools
import math

import jax
import jax.numpy as jnp
from jax import lax
from jax.experimental import pallas as pl
from jax.experimental.pallas import tpu as pltpu
from jax.sharding import PartitionSpec as P

EDGE = 128
GROUP = 32
PAD = 176
NY, NZ = 4, 8
F32, BF16 = jnp.float32, jnp.bfloat16
VMEM = pl.BlockSpec(memory_space=pltpu.VMEM)
SMEM = pl.BlockSpec(memory_space=pltpu.SMEM)
ANY = pl.BlockSpec(memory_space=pl.ANY)
HBM = pl.BlockSpec(memory_space=pltpu.HBM)
NT = (((1,), (1,)), ((), ()))


def dot(a, b):
    return jnp.dot(a, b, preferred_element_type=F32)


def dot_nt(a, b):
    return lax.dot_general(a, b, NT, preferred_element_type=F32)


def call(body, out, specs, scratch=(), mib=4, flops=0, bytes_accessed=0):
    return pl.pallas_call(
        body,
        out_shape=out,
        in_specs=specs,
        out_specs=jax.tree.map(lambda _: VMEM, out),
        scratch_shapes=list(scratch),
        compiler_params=pltpu.CompilerParams(vmem_limit_bytes=mib * 1024 * 1024),
        cost_estimate=pl.CostEstimate(
            flops=flops, bytes_accessed=bytes_accessed, transcendentals=0
        ),
    )


def step(x, groups, shift):
    pairs = [(g[i], g[(i + shift) % len(g)]) for g in groups for i in range(len(g))]
    return lax.ppermute(x, "row", pairs)


ALONG_Z = [[NZ * y + z for z in range(NZ)] for y in range(NY)]
ALONG_Y = [[NZ * y + z for y in range(NY)] for z in range(NZ)]


def ring(x, groups):
    count = len(groups[0])
    up = down = x
    parts = [x]
    for _ in range(count // 2 - 1):
        up, down = step(up, groups, 1), step(down, groups, -1)
        parts += [up, down]
    half = x.shape[0] // 2
    return parts + [step(up[:half], groups, 1), step(down[half:], groups, -1)]


def along_y(x):
    return [x, step(x, ALONG_Y, 1), step(x, ALONG_Y, -1), step(x, ALONG_Y, 2)]


def place_of(block, row):
    owner = block // 2
    dz = (owner % NZ + NZ - row % NZ) % NZ
    dy = (owner // NZ + NY - row // NZ) % NY
    z_place = jnp.where(dz <= 3, 2 * dz, jnp.where(dz == 4, 7, 15 - 2 * dz))
    y_place = jnp.where(dy == 0, 0, jnp.where(dy == 3, 1, dy + 1))
    return z_place * NY + y_place


def slot_of(block, col):
    owner = block // 2
    dx = (owner // 2 + 4 - col // 2) % 4
    dc = (owner + col) % 2
    return (dc * 4 + dx) * 2 + block % 2


def to_sibling(x):
    return lax.ppermute(x, "col", [(i, i ^ 1) for i in range(8)])


def along_x(x, shift):
    return lax.ppermute(x, "col", [(i, (i + 2 * shift) % 8) for i in range(8)])


def start_parts(parts, held, sems):
    copies, at = [], 0
    for i, p in enumerate(parts):
        n = p.shape[0]
        copies.append(pltpu.make_async_copy(p, held.at[pl.ds(at, n)], sems.at[i]))
        copies[-1].start()
        at += n
    return copies


def start_pairs(feat_parts, agg_parts, held, sems):
    copies, at = [], 0
    for i, pair in enumerate(zip(feat_parts, agg_parts)):
        n = pair[0].shape[0]
        for j, p in enumerate(pair):
            to = held.at[pl.ds(at, n), :, pl.ds(j * EDGE, EDGE)]
            copies.append(pltpu.make_async_copy(p, to, sems.at[2 * i + j]))
            copies[-1].start()
        at += n
    return copies


def start_tiles(tiles, held, sems):
    copies = []
    for i in range(held.shape[0] // GROUP):
        at = pl.ds(i * GROUP, GROUP)
        copies.append(pltpu.make_async_copy(tiles.at[at], held.at[at], sems.at[i]))
        copies[-1].start()
    return copies


def start_all(pairs, sems):
    copies = [pltpu.make_async_copy(a, b, sems.at[i]) for i, (a, b) in enumerate(pairs)]
    for c in copies:
        c.start()
    return copies


def accumulate(tiles, held, sems, product, add):
    def body(i, carry):
        at = pl.ds(i * GROUP, GROUP)
        pltpu.make_async_copy(tiles.at[at], held.at[at], sems.at[i]).wait()
        got = [product(i * GROUP + u) for u in range(GROUP)]
        for u in range(GROUP):
            add(i * GROUP + u, got[u])
        return carry

    lax.fori_loop(0, held.shape[0] // GROUP, body, 0)


def degree_kernel(first, slots, tiles, out, held, sem):
    tiles = tiles.at[pl.ds(first, GROUP)]
    start_tiles(tiles, held, sem)
    out[...] = jnp.zeros_like(out)
    ones = jnp.ones((8, EDGE), BF16)

    def product(t):
        x = held[t].astype(F32)
        x = x * x
        hi = x.astype(BF16)
        lo = (x - hi.astype(F32)).astype(BF16)
        return dot_nt(ones, hi) + dot_nt(ones, lo)

    def add(t, got):
        out[slots[first + t]] += got

    accumulate(tiles, held, sem, product, add)


def first_kernel(n_parts, offs, cols, tiles_hbm, d0, d1, d2, d3, *refs):
    parts, keep, send, tiles, held, acc, tile_sem, sem = refs[:n_parts], *refs[n_parts:]
    copies = start_parts(parts, held, sem)
    start_tiles(tiles_hbm, tiles, tile_sem)
    acc[...] = jnp.zeros_like(acc)
    for s in range(16):
        deg = (d0[s][:1] + d1[s][:1]) + (d2[s][:1] + d3[s][:1])
        acc[pl.ds(s // 2 * 264 + 256 + s % 2, 1), :] = deg
    for c in copies:
        c.wait()

    def add(t, got):
        acc[pl.ds(pl.multiple_of(offs[t], 8), EDGE), :] += got

    accumulate(tiles_hbm, tiles, tile_sem, lambda t: dot(tiles[t], held[cols[t]]), add)
    keep[...] = acc[pl.ds(0, 1056), :]
    send[...] = acc[pl.ds(1056, 1056), :]


def join_first_kernel(keep, got, *out):
    for x in range(4):
        at = pl.ds(x * 264, 264)
        out[x][...] = keep[at, :] + got[at, :]


def flip(x):
    return x.astype(F32).T


def flip(x):
    return x.astype(F32).T


def pre_first(weights_t, bias_t, both):
    return dot_nt(weights_t, both) + bias_t


def aggregate_kernel(s0, s1, s2, s3, agg, inv):
    total = (s0[...] + s1[...]) + (s2[...] + s3[...])
    for b in range(2):
        x = 1.0 + total[256 + b : 257 + b]
        r = lax.rsqrt(x)
        r = r * (1.5 - 0.5 * x * r * r)
        inv[pl.ds(b, 1), :] = r
        column = jnp.broadcast_to(r, (EDGE, EDGE)).T
        agg[b] = (column * total[b * EDGE : (b + 1) * EDGE]).astype(BF16)


def second_kernel(n_parts, slots, cols, tiles_hbm, neigh_hbm, weights, bias, *refs):
    feat_parts, agg_parts = refs[:n_parts], refs[n_parts : 2 * n_parts]
    agg, keep, send, mine, tiles, neigh, both, held, acc, tile_sem, sem, neigh_sem = refs[2 * n_parts :]
    copies = start_pairs(feat_parts, agg_parts, both, sem)
    start_tiles(tiles_hbm, tiles, tile_sem)
    neigh_copy = pltpu.make_async_copy(neigh_hbm, neigh, neigh_sem)
    neigh_copy.start()
    acc[...] = jnp.zeros_like(acc)
    weights_t = flip(weights[...]).astype(BF16)
    wide = 4
    bias_t = jnp.broadcast_to(bias[...], (wide * EDGE, bias.shape[1])).T
    for c in copies:
        c.wait()

    def hidden(i, carry):
        x = both[pl.ds(i * wide, wide)].reshape(wide * EDGE, 2 * EDGE)
        h = jnp.maximum(pre_first(weights_t, bias_t, x), 0.0).astype(BF16)
        for q in range(wide):
            held[i * wide + q] = h[:, q * EDGE : (q + 1) * EDGE]
        return carry

    lax.fori_loop(0, 64 // wide, hidden, 0, unroll=2)
    mine[...] = held[pl.ds(0, 2)]

    def add(t, got):
        acc[slots[t]] += got

    accumulate(tiles_hbm, tiles, tile_sem, lambda t: dot_nt(held[cols[t]], tiles[t]), add)
    neigh_copy.wait()
    for s in range(16):
        agg[s] = acc[s].astype(BF16)
        got = dot(neigh[pl.ds(0, PAD), :], agg[s]).astype(BF16)
        if s < 8:
            keep[s] = got
        else:
            send[s - 8] = got


def join_second_kernel(keep, got, *out):
    for s in range(8):
        out[s // 2][s % 2] = (keep[s].astype(F32) + got[s].astype(F32)).astype(BF16)


def loss_kernel(
    classes, scale, s0, s1, s2, s3, hid, self_t, bias, labels, mask, inv, lg, w, grad, grad_bias
):
    rows = lax.broadcasted_iota(jnp.int32, (PAD, EDGE), 0)
    ones = jnp.ones((8, EDGE), BF16)
    for b in range(2):
        total = (s0[b].astype(F32) + s1[b].astype(F32)) + (s2[b].astype(F32) + s3[b].astype(F32))
        factor = inv[b : b + 1]
        logits = dot(self_t[pl.ds(0, PAD), :], hid[b]) + factor * total + bias[...]
        logits = jnp.where(rows < classes, logits, -1e30)
        e = jnp.exp(logits - jnp.max(logits, axis=0, keepdims=True))
        p = e / jnp.sum(e, axis=0, keepdims=True)
        p = p - jnp.where(rows == labels[b : b + 1], 1.0, 0.0)
        got = (p * (mask[b : b + 1].astype(F32) * scale)).astype(BF16)
        lg[b] = got
        w[b] = (got.astype(F32) * factor).astype(BF16)
        if b == 0:
            grad[...] = dot_nt(got, hid[b])
            grad_bias[...] = dot_nt(ones, got)
        else:
            grad[...] += dot_nt(got, hid[b])
            grad_bias[...] += dot_nt(ones, got)


X_ORDER = (0, 3, 1, 2)


def last_kernel(
    n_parts, slots, cols, w0, w1, w2, w3, weights, bias, tiles_hbm, agg_second_hbm, lg_hbm, self_hbm,
    neigh_hbm, grad_self_hbm, grad_bias, *refs
):
    feat_parts, agg_parts = refs[:n_parts], refs[n_parts : 2 * n_parts]
    (
        out, tiles, agg_second, lg, self_t, neigh_t, grad_self, both, acc, proj,
        tile_sem, both_sem, sems,
    ) = refs[2 * n_parts :]
    pairs = (
        (neigh_hbm, neigh_t),
        (agg_second_hbm, agg_second),
        (lg_hbm, lg),
        (self_hbm, self_t),
        (grad_self_hbm, grad_self),
    )
    small = start_all(pairs, sems)
    start_tiles(tiles_hbm, tiles, tile_sem)
    copies = start_pairs(feat_parts, agg_parts, both, both_sem)
    acc[...] = jnp.zeros_like(acc)
    weights_t = flip(weights[...]).astype(BF16)
    for c in small:
        c.wait()
    lacking = jnp.zeros((256 - PAD, EDGE), BF16)
    self_second = flip(self_t[...]).astype(BF16)
    neigh_second = flip(neigh_t[...]).astype(BF16)
    for b in range(2):
        acc[b] = dot(self_second, jnp.concatenate([lg[b], lacking], axis=0))
    g_neigh = jnp.zeros((PAD, 256), F32)
    for dx, part in zip(X_ORDER, (w0, w1, w2, w3)):
        at = [(i // 2 * 4 + dx) * 2 + i % 2 for i in range(4)]
        w = jnp.concatenate([part[i] for i in range(4)], axis=1)
        tall = jnp.concatenate([w, jnp.concatenate([lacking] * 4, axis=1)], axis=0)
        got = dot(neigh_second, tall).astype(BF16)
        for i in range(4):
            proj[at[i]] = got[:, i * EDGE : (i + 1) * EDGE]
        g_neigh += dot_nt(w, jnp.concatenate([agg_second[s] for s in at], axis=1))
    for i in range(2):
        lanes = slice(i * EDGE, (i + 1) * EDGE)
        out[pl.ds(512 + i * PAD, PAD), :] = grad_self[:, lanes].astype(BF16)
        out[pl.ds(512 + (2 + i) * PAD, PAD), :] = g_neigh[:, lanes].astype(BF16)

    def add(t, got):
        acc[cols[t]] += got

    accumulate(tiles_hbm, tiles, tile_sem, lambda t: dot(proj[slots[t]], tiles[t]), add)
    for c in copies:
        c.wait()
    wide = 8
    ones = jnp.ones((8, wide * EDGE), BF16)
    bias_t = jnp.broadcast_to(bias[...], (wide * EDGE, bias.shape[1])).T

    def contract(i, carry):
        g_first, g_bias = carry
        x = both[pl.ds(i * wide, wide)].reshape(wide * EDGE, 2 * EDGE)
        back = jnp.concatenate([acc[i * wide + q] for q in range(wide)], axis=1)
        p = jnp.where(pre_first(weights_t, bias_t, x) > 0.0, back, 0.0).astype(BF16)
        return g_first + dot(p, x), g_bias + dot_nt(ones, p)

    zeros = (jnp.zeros((256, 256), F32), jnp.zeros((8, 256), F32))
    g_first, g_bias = lax.fori_loop(0, 64 // wide, contract, zeros)
    out[pl.ds(0, 256), :] = g_first[:, :EDGE].astype(BF16)
    out[pl.ds(256, 256), :] = g_first[:, EDGE:].astype(BF16)
    pick = lax.broadcasted_iota(jnp.int32, (16, EDGE), 0)
    second = jnp.concatenate([grad_bias[:1], jnp.zeros((1, 256 - PAD), F32)], axis=1)
    rows = (g_bias[:1, :EDGE], g_bias[:1, EDGE:], second[:, :EDGE], second[:, EDGE:])
    last = jnp.zeros((16, EDGE), F32)
    for i, row in enumerate(rows):
        last = jnp.where(pick == i, row, last)
    end = 512 + 4 * PAD
    out[pl.ds(end, 16), :] = last.astype(BF16)
    out[pl.ds(end + 16, 1280 - 16 - end), :] = jnp.zeros((1280 - 16 - end, EDGE), BF16)


def add_pieces_kernel(x, out):
    total = x[0].astype(F32)
    for i in range(1, x.shape[0]):
        total = total + x[i].astype(F32)
    out[...] = total.astype(BF16)


def spread_kernel(a, b, out):
    total = (a[...].astype(F32) + b[...].astype(F32)).astype(BF16)
    for i in range(out.shape[0]):
        out[i] = total


def unpack_kernel(classes, x, self_first, neigh_first, bias_first, self_t, neigh_t, bias_second):
    self_first[...] = flip(x[pl.ds(0, 256), :])
    neigh_first[...] = flip(x[pl.ds(256, 256), :])
    for at, out in ((512, self_t), (512 + 2 * PAD, neigh_t)):
        for i in range(2):
            got = x[pl.ds(at + i * PAD, PAD), :].astype(F32)
            out[:, i * EDGE : (i + 1) * EDGE] = got[:classes]
    last = x[pl.ds(512 + 4 * PAD, 16), :].astype(F32)
    bias_first[...] = jnp.concatenate([last[0:1], last[1:2]], axis=1)
    bias_second[...] = jnp.concatenate([last[2:3], last[3:4]], axis=1)


def sum_everywhere(x):
    every = ("row", "col")
    number = lambda y, z, x, c: ((y * NZ + z) * 4 + x) * 2 + c
    groups = [
        [number(y, z, x, c) for y in range(NY) for x in range(4)] for z in range(NZ) for c in range(2)
    ]
    x = x.reshape(16, -1, EDGE)
    piece = jax.ShapeDtypeStruct(x.shape[1:], BF16)
    x = lax.all_to_all(x, every, 0, 0, tiled=True, axis_index_groups=groups)
    x = call(add_pieces_kernel, piece, [VMEM])(x)
    x = jnp.broadcast_to(x[None], (NZ,) + x.shape)
    x = lax.all_to_all(x, "row", 0, 0, tiled=True, axis_index_groups=ALONG_Z)
    x = call(add_pieces_kernel, piece, [VMEM])(x)
    x = call(spread_kernel, jax.ShapeDtypeStruct((16, 80, EDGE), BF16), [VMEM] * 2)(x, to_sibling(x))
    x = lax.all_to_all(x, every, 0, 0, tiled=True, axis_index_groups=groups)
    return x.reshape(-1, EDGE)


def on_device(
    features,
    tiles,
    block_rows,
    block_cols,
    labels,
    train_mask,
    self_first,
    neigh_first,
    bias_first,
    self_second,
    neigh_second,
    bias_second,
):
    classes = self_second.shape[1]
    hid_size = self_first.shape[1]
    scale = 1.0 / math.sqrt(65536)
    row, col = lax.axis_index("row"), lax.axis_index("col")
    tiles = tiles.reshape(-1, EDGE, EDGE)
    slots = slot_of(block_rows.reshape(-1), col)
    sources = block_cols.reshape(-1)
    cols = place_of(sources, row) * 2 + sources % 2
    offs = slots // 2 * 264 + slots % 2 * EDGE
    shape = jax.ShapeDtypeStruct
    dma = pltpu.SemaphoreType.DMA
    feat = features.reshape(2, EDGE, EDGE)
    tile_buffer = pltpu.VMEM(tiles.shape, BF16)
    n_groups = tiles.shape[0] // GROUP

    feat_parts = ring(jnp.concatenate(along_y(feat), axis=0), ALONG_Z)
    n_feat = len(feat_parts)
    degs = [
        call(
            functools.partial(degree_kernel, i * GROUP),
            shape((16, 8, EDGE), F32),
            [SMEM, HBM],
            [pltpu.VMEM((GROUP, EDGE, EDGE), BF16), dma((1,))],
            mib=60,
            flops=2**32,
            bytes_accessed=2**20,
        )(slots, tiles)
        for i in range(n_groups)
    ]
    block = shape((1056, EDGE), F32)
    keep, send = call(
        functools.partial(first_kernel, n_feat),
        (block, block),
        [SMEM, SMEM, HBM] + [VMEM] * 4 + [ANY] * n_feat,
        [
            tile_buffer,
            pltpu.VMEM((64, EDGE, EDGE), BF16),
            pltpu.VMEM((2112, EDGE), F32),
            dma((n_groups,)),
            dma((n_feat,)),
        ],
        mib=60,
        flops=2**29,
        bytes_accessed=2**23,
    )(offs, cols, tiles, *degs, *feat_parts)
    sums = call(join_first_kernel, (shape((264, EDGE), F32),) * 4, [VMEM] * 2)(
        keep, to_sibling(send)
    )
    agg, inv = call(
        aggregate_kernel, (shape((2, EDGE, EDGE), BF16), shape((2, EDGE), F32)), [VMEM] * 4
    )(sums[0], along_x(sums[1], 1), along_x(sums[2], 2), along_x(sums[3], 3))
    agg_parts = ring(jnp.concatenate(along_y(agg), axis=0), ALONG_Z)
    weights = jnp.concatenate([self_first, neigh_first], axis=0)
    bias = bias_first.reshape(1, -1)

    lacking = ((0, 256 - classes), (0, 0))
    self_t = jnp.pad(self_second.T, lacking)
    neigh_t = jnp.pad(neigh_second.T, lacking)
    bias_wide = jnp.broadcast_to(jnp.pad(bias_second, (0, PAD - classes))[:, None], (PAD, EDGE))
    half = shape((8, PAD, EDGE), BF16)
    agg_second, keep, send, hid = call(
        functools.partial(second_kernel, n_feat),
        (shape((16, hid_size, EDGE), BF16), half, half, shape((2, hid_size, EDGE), BF16)),
        [SMEM, SMEM, HBM, HBM, VMEM, VMEM] + [HBM] * (2 * n_feat),
        [
            tile_buffer,
            pltpu.VMEM((256, hid_size), BF16),
            pltpu.VMEM((64, EDGE, 2 * EDGE), BF16),
            pltpu.VMEM((64, hid_size, EDGE), BF16),
            pltpu.VMEM((16, hid_size, EDGE), F32),
            dma((n_groups,)),
            dma((2 * n_feat,)),
            dma(()),
        ],
        mib=60,
        flops=2**31,
        bytes_accessed=2**23,
    )(slots, cols, tiles, neigh_t, weights, bias, *feat_parts, *agg_parts)
    sums = call(join_second_kernel, (shape((2, PAD, EDGE), BF16),) * 4, [VMEM] * 2)(
        keep, to_sibling(send)
    )
    lg, w, grad_self, grad_bias = call(
        functools.partial(loss_kernel, classes, scale),
        (
            shape((2, PAD, EDGE), BF16),
            shape((2, PAD, EDGE), BF16),
            shape((PAD, hid_size), F32),
            shape((8, PAD), F32),
        ),
        [VMEM] * 10,
    )(
        sums[0],
        along_x(sums[1], 1),
        along_x(sums[2], 2),
        along_x(sums[3], 3),
        hid,
        self_t,
        bias_wide,
        labels.reshape(2, EDGE),
        train_mask.reshape(2, EDGE),
        inv,
    )
    w = jnp.concatenate([w, to_sibling(w)], axis=0)
    w_parts = [w, along_x(w, 1), along_x(w, 3), along_x(w, 2)]
    grads = call(
        functools.partial(last_kernel, n_feat),
        shape((1280, EDGE), BF16),
        [SMEM] * 2 + [VMEM] * 6 + [HBM] * 6 + [VMEM] + [HBM] * (2 * n_feat),
        [
            tile_buffer,
            pltpu.VMEM((16, hid_size, EDGE), BF16),
            pltpu.VMEM((2, PAD, EDGE), BF16),
            pltpu.VMEM((256, hid_size), BF16),
            pltpu.VMEM((256, hid_size), BF16),
            pltpu.VMEM((PAD, hid_size), F32),
            pltpu.VMEM((64, EDGE, 2 * EDGE), BF16),
            pltpu.VMEM((64, hid_size, EDGE), F32),
            pltpu.VMEM((16, hid_size, EDGE), BF16),
            dma((n_groups,)),
            dma((2 * n_feat,)),
            dma((5,)),
        ],
        mib=60,
        flops=2**31,
        bytes_accessed=2**24,
    )(
        slots, cols, *w_parts, weights, bias, tiles, agg_second, lg, self_t, neigh_t, grad_self,
        grad_bias, *feat_parts, *agg_parts
    )
    out = call(
        functools.partial(unpack_kernel, classes),
        (
            shape(self_first.shape, F32),
            shape(neigh_first.shape, F32),
            shape((1, hid_size), F32),
            shape((classes, hid_size), F32),
            shape((classes, hid_size), F32),
            shape((1, 256), F32),
        ),
        [VMEM],
    )(sum_everywhere(grads))
    return (
        out[0],
        out[1],
        out[2].reshape(hid_size),
        out[3].T,
        out[4].T,
        out[5].reshape(256)[:classes],
    )


def solution(mesh):
    in_specs = (
        P(("row", "col"), None),
        P("row", "col", None, None, None),
        P("row", "col", None),
        P("row", "col", None),
        P(("row", "col")),
        P(("row", "col")),
        P(),
        P(),
        P(),
        P(),
        P(),
        P(),
    )
    out_specs = (P(), P(), P(), P(), P(), P())
    return jax.shard_map(
        on_device, mesh=mesh, in_specs=in_specs, out_specs=out_specs, check_vma=False
    )
```

profile of v0, /device:TPU:1, one launch (start us, length us, event | category | flops | bytes accessed | tf_op | source)
XLA Modules:
  0.0 207.0 jit_solution(16162130434001043262)
XLA Ops:
  0.6 3.8 %collective-permute-start.2 = (bf16[2,128,128]{2,1,0:T(8,128)(2,1)}, bf16[2,128,128]{2,1,0:T(8,128)(2,1)S(1)}, u32[]{:S(2)}, u32[]{:S(2)}) collective-permute-start(bf16[2,128,128]{2,1,0:T(8,128)(2,1)} %bitcast.54), channel_id=1, source_target_pairs={{0,128},{64,192},{128,0},{192,64},{8,136},{72,200},{136,8},{200,72... | collective-permute-start | bytes 196616 | tf_op jit(solution)/shard_map/ppermute | solution.py:47
  10.8 5.5 %collective-permute-start.4 = (bf16[8,128,128]{2,1,0:T(8,128)(2,1)S(1)}, bf16[8,128,128]{2,1,0:T(8,128)(2,1)S(1)}, u32[]{:S(2)}, u32[]{:S(2)}) collective-permute-start(bf16[8,128,128]{2,1,0:T(8,128)(2,1)S(1)} %pad_maximum_fusion.refs_0_), channel_id=1, source_target_pairs={{0,56},{8,0},{16,8},{24,16},{32,24},{40,32},{48,40},{56,48},{64,12... | collective-permute-start | bytes 786440 | tf_op jit(solution)/shard_map/ppermute | solution.py:47
  16.3 3.7 %shard_map.166.d3 = f32[16,8,128]{2,1,0:T(8,128)} custom-call(s32[128]{0:T(128)} %get-tuple-element.59.slots, bf16[128,128,128]{2,1,0:T(8,128)(2,1)} %bitcast.44), custom_call_target="tpu_custom_call" | custom-call | flops 4294967296 | bytes 1048576 | tf_op jit(solution)/shard_map/pallas_call | solution.py:429
  20.1 2.8 %collective-permute-start.6 = (bf16[8,128,128]{2,1,0:T(8,128)(2,1)S(1)}, bf16[8,128,128]{2,1,0:T(8,128)(2,1)S(1)}, u32[]{:S(2)}, u32[]{:S(2)}) collective-permute-start(bf16[8,128,128]{2,1,0:T(8,128)(2,1)S(1)} %collective-permute-done.4.refs_2_), channel_id=1, source_target_pairs={{0,56},{8,0},{16,8},{24,16},{32,24},{40,32},{48,40},{56,48},{64,12... | collective-permute-start | bytes 786440 | tf_op jit(solution)/shard_map/ppermute | solution.py:47
  22.9 3.7 %shard_map.165.d2 = f32[16,8,128]{2,1,0:T(8,128)} custom-call(s32[128]{0:T(128)} %get-tuple-element.59.slots, bf16[128,128,128]{2,1,0:T(8,128)(2,1)} %bitcast.45), custom_call_target="tpu_custom_call" | custom-call | flops 4294967296 | bytes 1048576 | tf_op jit(solution)/shard_map/pallas_call | solution.py:429
  26.6 2.7 %collective-permute-start.8 = (bf16[8,128,128]{2,1,0:T(8,128)(2,1)S(1)}, bf16[8,128,128]{2,1,0:T(8,128)(2,1)S(1)}, u32[]{:S(2)}, u32[]{:S(2)}) collective-permute-start(bf16[8,128,128]{2,1,0:T(8,128)(2,1)S(1)} %collective-permute-done.6.refs_4_), channel_id=1, source_target_pairs={{0,56},{8,0},{16,8},{24,16},{32,24},{40,32},{48,40},{56,48},{64,12... | collective-permute-start | bytes 786440 | tf_op jit(solution)/shard_map/ppermute | solution.py:47
  29.4 3.7 %shard_map.164.d1 = f32[16,8,128]{2,1,0:T(8,128)} custom-call(s32[128]{0:T(128)} %get-tuple-element.59.slots, bf16[128,128,128]{2,1,0:T(8,128)(2,1)} %bitcast.46), custom_call_target="tpu_custom_call" | custom-call | flops 4294967296 | bytes 1048576 | tf_op jit(solution)/shard_map/pallas_call | solution.py:429
  33.2 2.9 %collective-permute-start.10 = (bf16[4,128,128]{2,1,0:T(8,128)(2,1)S(1)}, bf16[4,128,128]{2,1,0:T(8,128)(2,1)S(1)}, u32[]{:S(2)}, u32[]{:S(2)}) collective-permute-start(bf16[4,128,128]{2,1,0:T(8,128)(2,1)S(1)} %slice.25), channel_id=1, source_target_pairs={{0,56},{8,0},{16,8},{24,16},{32,24},{40,32},{48,40},{56,48},{64,12... | collective-permute-start | bytes 393224 | tf_op jit(solution)/shard_map/ppermute | solution.py:47
  36.6 3.7 %shard_map.163.d0 = f32[16,8,128]{2,1,0:T(8,128)} custom-call(s32[128]{0:T(128)} %get-tuple-element.59.slots, bf16[128,128,128]{2,1,0:T(8,128)(2,1)} %bitcast.47), custom_call_target="tpu_custom_call" | custom-call | flops 4294967296 | bytes 1048576 | tf_op jit(solution)/shard_map/pallas_call | solution.py:429
  40.3 2.6 %collective-permute-done.9.refs_7_ = bf16[4,128,128]{2,1,0:T(8,128)(2,1)S(1)} collective-permute-done((bf16[4,128,128]{2,1,0:T(8,128)(2,1)S(1)}, bf16[4,128,128]{2,1,0:T(8,128)(2,1)S(1)}, u32[]{:S(2)}, u32[]{:S(2)}) %collective-permute-start.9) | collective-permute-done | bytes 131104 | tf_op jit(solution)/shard_map/ppermute | solution.py:47
  43.6 6.5 %shard_map.167 = (f32[1056,128]{1,0:T(8,128)}, f32[1056,128]{1,0:T(8,128)}) custom-call(s32[128]{0:T(128)} %get-tuple-element.58.offs, s32[128]{0:T(128)} %get-tuple-element.60.cols, bf16[128,128,128]{2,1,0:T(8,128)(2,1)} %bitcast.48, f32[16,8,128]{2,1,0:T(8,128)} %shard_map.163.d0, f32[16,8,128]{2,1,0:T(8,128)} %shard_map.164.d1, ...), custom_call_target="tpu_custom_call" | custom-call | flops 536870912 | bytes 8388608 | tf_op jit(solution)/shard_map/pallas_call | solution.py:441
  50.1 6.9 %collective-permute-start.11 = (f32[1056,128]{1,0:T(8,128)}, f32[1056,128]{1,0:T(8,128)S(1)}, u32[]{:S(2)}, u32[]{:S(2)}) collective-permute-start(f32[1056,128]{1,0:T(8,128)} %get-tuple-element.33), channel_id=1, source_target_pairs={{0,1},{1,0},{2,3},{3,2},{4,5},{5,4},{6,7},{7,6},{8,9},{9,8},{10,11... | collective-permute-start | bytes 1622024 | tf_op jit(solution)/shard_map/ppermute | solution.py:86
  61.2 2.4 %collective-permute-start.13 = (f32[264,128]{1,0:T(8,128)S(1)}, f32[264,128]{1,0:T(8,128)S(1)}, u32[]{:S(2)}, u32[]{:S(2)}) collective-permute-start(f32[264,128]{1,0:T(8,128)S(1)} %get-tuple-element.36), channel_id=1, source_target_pairs={{0,4},{1,5},{2,6},{3,7},{4,0},{5,1},{6,2},{7,3},{8,12},{9,13},{10,... | collective-permute-start | bytes 405512 | tf_op jit(solution)/shard_map/ppermute | solution.py:90
  66.0 3.9 %collective-permute-done.13.s2 = f32[264,128]{1,0:T(8,128)S(1)} collective-permute-done((f32[264,128]{1,0:T(8,128)S(1)}, f32[264,128]{1,0:T(8,128)S(1)}, u32[]{:S(2)}, u32[]{:S(2)}) %collective-permute-start.13) | collective-permute-done | bytes 135200 | tf_op jit(solution)/shard_map/ppermute | solution.py:90
  71.7 4.5 %collective-permute-done.15 = bf16[2,128,128]{2,1,0:T(8,128)(2,1)S(1)} collective-permute-done((bf16[2,128,128]{2,1,0:T(8,128)(2,1)S(1)}, bf16[2,128,128]{2,1,0:T(8,128)(2,1)S(1)}, u32[]{:S(2)}, u32[]{:S(2)}) %collective-permute-start.15) | collective-permute-done | bytes 65568 | tf_op jit(solution)/shard_map/ppermute | solution.py:47
  77.8 3.8 %collective-permute-done.19.refs_11_ = bf16[8,128,128]{2,1,0:T(8,128)(2,1)S(1)} collective-permute-done((bf16[8,128,128]{2,1,0:T(8,128)(2,1)S(1)}, bf16[8,128,128]{2,1,0:T(8,128)(2,1)S(1)}, u32[]{:S(2)}, u32[]{:S(2)}) %collective-permute-start.19) | collective-permute-done | bytes 262176 | tf_op jit(solution)/shard_map/ppermute | solution.py:47
  83.4 3.9 %collective-permute-done.21.refs_13_ = bf16[8,128,128]{2,1,0:T(8,128)(2,1)S(1)} collective-permute-done((bf16[8,128,128]{2,1,0:T(8,128)(2,1)S(1)}, bf16[8,128,128]{2,1,0:T(8,128)(2,1)S(1)}, u32[]{:S(2)}, u32[]{:S(2)}) %collective-permute-start.21) | collective-permute-done | bytes 262176 | tf_op jit(solution)/shard_map/ppermute | solution.py:47
  87.3 2.5 %collective-permute-start.23 = (bf16[8,128,128]{2,1,0:T(8,128)(2,1)S(1)}, bf16[8,128,128]{2,1,0:T(8,128)(2,1)S(1)}, u32[]{:S(2)}, u32[]{:S(2)}) collective-permute-start(bf16[8,128,128]{2,1,0:T(8,128)(2,1)S(1)} %collective-permute-done.21.refs_13_), channel_id=1, source_target_pairs={{0,56},{8,0},{16,8},{24,16},{32,24},{40,32},{48,40},{56,48},{64,12... | collective-permute-start | bytes 786440 | tf_op jit(solution)/shard_map/ppermute | solution.py:47
  89.9 4.6 %collective-permute-done.23.refs_15_ = bf16[8,128,128]{2,1,0:T(8,128)(2,1)S(1)} collective-permute-done((bf16[8,128,128]{2,1,0:T(8,128)(2,1)S(1)}, bf16[8,128,128]{2,1,0:T(8,128)(2,1)S(1)}, u32[]{:S(2)}, u32[]{:S(2)}) %collective-permute-start.23) | collective-permute-done | bytes 262176 | tf_op jit(solution)/shard_map/ppermute | solution.py:47
  94.5 2.3 %collective-permute-start.25 = (bf16[4,128,128]{2,1,0:T(8,128)(2,1)S(1)}, bf16[4,128,128]{2,1,0:T(8,128)(2,1)S(1)}, u32[]{:S(2)}, u32[]{:S(2)}) collective-permute-start(bf16[4,128,128]{2,1,0:T(8,128)(2,1)S(1)} %slice.27), channel_id=1, source_target_pairs={{0,56},{8,0},{16,8},{24,16},{32,24},{40,32},{48,40},{56,48},{64,12... | collective-permute-start | bytes 393224 | tf_op jit(solution)/shard_map/ppermute | solution.py:47
  100.2 3.9 %collective-permute-done.24.refs_16_ = bf16[4,128,128]{2,1,0:T(8,128)(2,1)S(1)} collective-permute-done((bf16[4,128,128]{2,1,0:T(8,128)(2,1)S(1)}, bf16[4,128,128]{2,1,0:T(8,128)(2,1)S(1)}, u32[]{:S(2)}, u32[]{:S(2)}) %collective-permute-start.24) | collective-permute-done | bytes 131104 | tf_op jit(solution)/shard_map/ppermute | solution.py:47
  104.8 11.4 %shard_map.170 = (bf16[16,256,128]{2,1,0:T(8,128)(2,1)}, bf16[8,176,128]{2,1,0:T(8,128)(2,1)}, bf16[8,176,128]{2,1,0:T(8,128)(2,1)}, bf16[2,256,128]{2,1,0:T(8,128)(2,1)}) custom-call(s32[128]{0:T(128)} %get-tuple-element.59.slots, s32[128]{0:T(128)} %get-tuple-element.60.cols, bf16[128,128,128]{2,1,0:T(8,128)(2,1)} %bitcast.49, ...), custom_call_target="tpu_custom_call" | custom-call | flops 2147483648 | bytes 8388608 | tf_op jit(solution)/shard_map/pallas_call | solution.py:471
  116.2 7.1 %collective-permute-start.26 = (bf16[8,176,128]{2,1,0:T(8,128)(2,1)}, bf16[8,176,128]{2,1,0:T(8,128)(2,1)S(1)}, u32[]{:S(2)}, u32[]{:S(2)}) collective-permute-start(bf16[8,176,128]{2,1,0:T(8,128)(2,1)} %get-tuple-element.40), channel_id=1, source_target_pairs={{0,1},{1,0},{2,3},{3,2},{4,5},{5,4},{6,7},{7,6},{8,9},{9,8},{10,11... | collective-permute-start | bytes 1081352 | tf_op jit(solution)/shard_map/ppermute | solution.py:86
  131.3 2.3 %collective-permute-done.28.s2 = bf16[2,176,128]{2,1,0:T(8,128)(2,1)S(1)} collective-permute-done((bf16[2,176,128]{2,1,0:T(8,128)(2,1)S(1)}, bf16[2,176,128]{2,1,0:T(8,128)(2,1)S(1)}, u32[]{:S(2)}, u32[]{:S(2)}) %collective-permute-start.28) | collective-permute-done | bytes 90144 | tf_op jit(solution)/shard_map/ppermute | solution.py:90
  139.4 3.2 %collective-permute-start.33 = (bf16[4,176,128]{2,1,0:T(8,128)(2,1)S(1)}, bf16[4,176,128]{2,1,0:T(8,128)(2,1)S(1)}, u32[]{:S(2)}, u32[]{:S(2)}) collective-permute-start(bf16[4,176,128]{2,1,0:T(8,128)(2,1)S(1)} %constant_dynamic-update-slice_fusion.6.w0), channel_id=1, source_target_pairs={{0,4},{1,5},{2,6},{3,7},{4,0},{5,1},{6,2},{7,3},{8,12},{9,13},{10,... | collective-permute-start | bytes 540680 | tf_op jit(solution)/shard_map/ppermute | solution.py:90
  144.0 3.0 %collective-permute-done.33.w3 = bf16[4,176,128]{2,1,0:T(8,128)(2,1)S(1)} collective-permute-done((bf16[4,176,128]{2,1,0:T(8,128)(2,1)S(1)}, bf16[4,176,128]{2,1,0:T(8,128)(2,1)S(1)}, u32[]{:S(2)}, u32[]{:S(2)}) %collective-permute-start.33) | collective-permute-done | bytes 180256 | tf_op jit(solution)/shard_map/ppermute | solution.py:90
  147.0 4.3 %collective-permute-done.32.w2 = bf16[4,176,128]{2,1,0:T(8,128)(2,1)S(1)} collective-permute-done((bf16[4,176,128]{2,1,0:T(8,128)(2,1)S(1)}, bf16[4,176,128]{2,1,0:T(8,128)(2,1)S(1)}, u32[]{:S(2)}, u32[]{:S(2)}) %collective-permute-start.32) | collective-permute-done | bytes 180256 | tf_op jit(solution)/shard_map/ppermute | solution.py:90
  152.1 14.9 %shard_map.173 = bf16[1280,128]{1,0:T(8,128)(2,1)} custom-call(s32[128]{0:T(128)} %get-tuple-element.59.slots, s32[128]{0:T(128)} %get-tuple-element.60.cols, bf16[4,176,128]{2,1,0:T(8,128)(2,1)} %copy-done.28, bf16[4,176,128]{2,1,0:T(8,128)(2,1)} %copy-done.31, bf16[4,176,128]{2,1,0:T(8,128)(2,1)} %copy-done.30, bf16[4,176,128]{2,1,0:T(8,128)(2,1)} %copy-done.29, ...), custom_call_target="tpu_custom_call" | custom-call | flops 2147483648 | bytes 16777216 | tf_op jit(solution)/shard_map/pallas_call | solution.py:515
  167.0 13.1 %all_to_all.15.x = bf16[16,80,128]{2,1,0:T(8,128)(2,1)S(1)} all-to-all(bf16[16,80,128]{2,1,0:T(8,128)(2,1)} %bitcast.51), channel_id=1, replica_groups={{0,2,4,6,64,66,68,70,128,130,132,134,192,194,196,198},{1,3,5,7,65,67,69..., dimensions={0} | all-to-all | bytes 655360 | tf_op jit(solution)/shard_map/all_to_all | solution.py:387
  180.2 10.8 %all_to_all.16.x = bf16[8,80,128]{2,1,0:T(8,128)(2,1)S(1)} all-to-all(bf16[8,80,128]{2,1,0:T(8,128)(2,1)S(1)} %broadcast_in_dim.9), channel_id=1, replica_groups={{0,8,16,24,32,40,48,56},{64,72,80,88,96,104,112,120},{128,136,144,152,1..., dimensions={0} | all-to-all | bytes 327680 | tf_op jit(solution)/shard_map/all_to_all | solution.py:390
  191.0 2.8 %collective-permute-start.34 = (bf16[80,128]{1,0:T(8,128)(2,1)S(1)}, bf16[80,128]{1,0:T(8,128)(2,1)S(1)}, u32[]{:S(2)}, u32[]{:S(2)}) collective-permute-start(bf16[80,128]{1,0:T(8,128)(2,1)S(1)} %shard_map.175.a), channel_id=1, source_target_pairs={{0,1},{1,0},{2,3},{3,2},{4,5},{5,4},{6,7},{7,6},{8,9},{9,8},{10,11... | collective-permute-start | bytes 61448 | tf_op jit(solution)/shard_map/ppermute | solution.py:86
  194.6 11.5 %all_to_all.17 = bf16[16,80,128]{2,1,0:T(8,128)(2,1)S(1)} all-to-all(bf16[16,80,128]{2,1,0:T(8,128)(2,1)S(1)} %shard_map.176), channel_id=1, replica_groups={{0,2,4,6,64,66,68,70,128,130,132,134,192,194,196,198},{1,3,5,7,65,67,69..., dimensions={0} | all-to-all | bytes 655360 | tf_op jit(solution)/shard_map/all_to_all | solution.py:393
  (149 shorter events, 41.0 us)
Async XLA Ops:
  0.6 6.5 %collective-permute-start.2 = (bf16[2,128,128]{2,1,0:T(8,128)(2,1)}, bf16[2,128,128]{2,1,0:T(8,128)(2,1)S(1)}, u32[]{:S(2)}, u32[]{:S(2)}) collective-permute-start(bf16[2,128,128]{2,1,0:T(8,128)(2,1)} %bitcast.54), channel_id=1, source_target_pairs={{0,128},{64,192},{128,0},{192,64},{8,136},{72,200},{136,8},{200,72... | collective-permute-start | bytes 196616 | tf_op jit(solution)/shard_map/ppermute | solution.py:47
  5.2 4.7 %collective-permute-start = (bf16[2,128,128]{2,1,0:T(8,128)(2,1)}, bf16[2,128,128]{2,1,0:T(8,128)(2,1)S(1)}, u32[]{:S(2)}, u32[]{:S(2)}) collective-permute-start(bf16[2,128,128]{2,1,0:T(8,128)(2,1)} %bitcast.56), channel_id=1, source_target_pairs={{0,64},{64,128},{128,192},{192,0},{8,72},{72,136},{136,200},{200,8... | collective-permute-start | bytes 196616 | tf_op jit(solution)/shard_map/ppermute | solution.py:47
  10.8 9.2 %collective-permute-start.4 = (bf16[8,128,128]{2,1,0:T(8,128)(2,1)S(1)}, bf16[8,128,128]{2,1,0:T(8,128)(2,1)S(1)}, u32[]{:S(2)}, u32[]{:S(2)}) collective-permute-start(bf16[8,128,128]{2,1,0:T(8,128)(2,1)S(1)} %pad_maximum_fusion.refs_0_), channel_id=1, source_target_pairs={{0,56},{8,0},{16,8},{24,16},{32,24},{40,32},{48,40},{56,48},{64,12... | collective-permute-start | bytes 786440 | tf_op jit(solution)/shard_map/ppermute | solution.py:47
  16.3 6.5 %collective-permute-start.3 = (bf16[8,128,128]{2,1,0:T(8,128)(2,1)S(1)}, bf16[8,128,128]{2,1,0:T(8,128)(2,1)S(1)}, u32[]{:S(2)}, u32[]{:S(2)}) collective-permute-start(bf16[8,128,128]{2,1,0:T(8,128)(2,1)S(1)} %pad_maximum_fusion.refs_0_), channel_id=1, source_target_pairs={{0,8},{8,16},{16,24},{24,32},{32,40},{40,48},{48,56},{56,0},{64,72... | collective-permute-start | bytes 786440 | tf_op jit(solution)/shard_map/ppermute | solution.py:47
  20.1 6.5 %collective-permute-start.6 = (bf16[8,128,128]{2,1,0:T(8,128)(2,1)S(1)}, bf16[8,128,128]{2,1,0:T(8,128)(2,1)S(1)}, u32[]{:S(2)}, u32[]{:S(2)}) collective-permute-start(bf16[8,128,128]{2,1,0:T(8,128)(2,1)S(1)} %collective-permute-done.4.refs_2_), channel_id=1, source_target_pairs={{0,56},{8,0},{16,8},{24,16},{32,24},{40,32},{48,40},{56,48},{64,12... | collective-permute-start | bytes 786440 | tf_op jit(solution)/shard_map/ppermute | solution.py:47
  22.9 6.5 %collective-permute-start.5 = (bf16[8,128,128]{2,1,0:T(8,128)(2,1)S(1)}, bf16[8,128,128]{2,1,0:T(8,128)(2,1)S(1)}, u32[]{:S(2)}, u32[]{:S(2)}) collective-permute-start(bf16[8,128,128]{2,1,0:T(8,128)(2,1)S(1)} %collective-permute-done.3.refs_1_), channel_id=1, source_target_pairs={{0,8},{8,16},{16,24},{24,32},{32,40},{40,48},{48,56},{56,0},{64,72... | collective-permute-start | bytes 786440 | tf_op jit(solution)/shard_map/ppermute | solution.py:47
  26.6 6.5 %collective-permute-start.8 = (bf16[8,128,128]{2,1,0:T(8,128)(2,1)S(1)}, bf16[8,128,128]{2,1,0:T(8,128)(2,1)S(1)}, u32[]{:S(2)}, u32[]{:S(2)}) collective-permute-start(bf16[8,128,128]{2,1,0:T(8,128)(2,1)S(1)} %collective-permute-done.6.refs_4_), channel_id=1, source_target_pairs={{0,56},{8,0},{16,8},{24,16},{32,24},{40,32},{48,40},{56,48},{64,12... | collective-permute-start | bytes 786440 | tf_op jit(solution)/shard_map/ppermute | solution.py:47
  29.4 6.9 %collective-permute-start.7 = (bf16[8,128,128]{2,1,0:T(8,128)(2,1)S(1)}, bf16[8,128,128]{2,1,0:T(8,128)(2,1)S(1)}, u32[]{:S(2)}, u32[]{:S(2)}) collective-permute-start(bf16[8,128,128]{2,1,0:T(8,128)(2,1)S(1)} %collective-permute-done.5.refs_3_), channel_id=1, source_target_pairs={{0,8},{8,16},{16,24},{24,32},{32,40},{40,48},{48,56},{56,0},{64,72... | collective-permute-start | bytes 786440 | tf_op jit(solution)/shard_map/ppermute | solution.py:47
  33.2 7.1 %collective-permute-start.10 = (bf16[4,128,128]{2,1,0:T(8,128)(2,1)S(1)}, bf16[4,128,128]{2,1,0:T(8,128)(2,1)S(1)}, u32[]{:S(2)}, u32[]{:S(2)}) collective-permute-start(bf16[4,128,128]{2,1,0:T(8,128)(2,1)S(1)} %slice.25), channel_id=1, source_target_pairs={{0,56},{8,0},{16,8},{24,16},{32,24},{40,32},{48,40},{56,48},{64,12... | collective-permute-start | bytes 393224 | tf_op jit(solution)/shard_map/ppermute | solution.py:47
  36.3 6.6 %collective-permute-start.9 = (bf16[4,128,128]{2,1,0:T(8,128)(2,1)S(1)}, bf16[4,128,128]{2,1,0:T(8,128)(2,1)S(1)}, u32[]{:S(2)}, u32[]{:S(2)}) collective-permute-start(bf16[4,128,128]{2,1,0:T(8,128)(2,1)S(1)} %slice.24), channel_id=1, source_target_pairs={{0,8},{8,16},{16,24},{24,32},{32,40},{40,48},{48,56},{56,0},{64,72... | collective-permute-start | bytes 393224 | tf_op jit(solution)/shard_map/ppermute | solution.py:47
  50.1 8.7 %collective-permute-start.11 = (f32[1056,128]{1,0:T(8,128)}, f32[1056,128]{1,0:T(8,128)S(1)}, u32[]{:S(2)}, u32[]{:S(2)}) collective-permute-start(f32[1056,128]{1,0:T(8,128)} %get-tuple-element.33), channel_id=1, source_target_pairs={{0,1},{1,0},{2,3},{3,2},{4,5},{5,4},{6,7},{7,6},{8,9},{9,8},{10,11... | collective-permute-start | bytes 1622024 | tf_op jit(solution)/shard_map/ppermute | solution.py:86
  59.9 6.1 %collective-permute-start.12 = (f32[264,128]{1,0:T(8,128)S(1)}, f32[264,128]{1,0:T(8,128)S(1)}, u32[]{:S(2)}, u32[]{:S(2)}) collective-permute-start(f32[264,128]{1,0:T(8,128)S(1)} %get-tuple-element.35), channel_id=1, source_target_pairs={{0,2},{1,3},{2,4},{3,5},{4,6},{5,7},{6,0},{7,1},{8,10},{9,11},{10,... | collective-permute-start | bytes 405512 | tf_op jit(solution)/shard_map/ppermute | solution.py:90
  61.2 8.7 %collective-permute-start.13 = (f32[264,128]{1,0:T(8,128)S(1)}, f32[264,128]{1,0:T(8,128)S(1)}, u32[]{:S(2)}, u32[]{:S(2)}) collective-permute-start(f32[264,128]{1,0:T(8,128)S(1)} %get-tuple-element.36), channel_id=1, source_target_pairs={{0,4},{1,5},{2,6},{3,7},{4,0},{5,1},{6,2},{7,3},{8,12},{9,13},{10,... | collective-permute-start | bytes 405512 | tf_op jit(solution)/shard_map/ppermute | solution.py:90
  63.7 6.2 %collective-permute-start.14 = (f32[264,128]{1,0:T(8,128)S(1)}, f32[264,128]{1,0:T(8,128)S(1)}, u32[]{:S(2)}, u32[]{:S(2)}) collective-permute-start(f32[264,128]{1,0:T(8,128)S(1)} %get-tuple-element.37), channel_id=1, source_target_pairs={{0,6},{1,7},{2,0},{3,1},{4,2},{5,3},{6,4},{7,5},{8,14},{9,15},{10,... | collective-permute-start | bytes 405512 | tf_op jit(solution)/shard_map/ppermute | solution.py:90
  70.0 6.2 %collective-permute-start.17 = (bf16[2,128,128]{2,1,0:T(8,128)(2,1)S(1)}, bf16[2,128,128]{2,1,0:T(8,128)(2,1)S(1)}, u32[]{:S(2)}, u32[]{:S(2)}) collective-permute-start(bf16[2,128,128]{2,1,0:T(8,128)(2,1)S(1)} %get-tuple-element.38), channel_id=1, source_target_pairs={{0,128},{64,192},{128,0},{192,64},{8,136},{72,200},{136,8},{200,72... | collective-permute-start | bytes 196616 | tf_op jit(solution)/shard_map/ppermute | solution.py:47
  70.1 6.0 %collective-permute-start.16 = (bf16[2,128,128]{2,1,0:T(8,128)(2,1)S(1)}, bf16[2,128,128]{2,1,0:T(8,128)(2,1)S(1)}, u32[]{:S(2)}, u32[]{:S(2)}) collective-permute-start(bf16[2,128,128]{2,1,0:T(8,128)(2,1)S(1)} %get-tuple-element.38), channel_id=1, source_target_pairs={{0,192},{64,0},{128,64},{192,128},{8,200},{72,8},{136,72},{200,136... | collective-permute-start | bytes 196616 | tf_op jit(solution)/shard_map/ppermute | solution.py:47
  71.4 4.7 %collective-permute-start.15 = (bf16[2,128,128]{2,1,0:T(8,128)(2,1)S(1)}, bf16[2,128,128]{2,1,0:T(8,128)(2,1)S(1)}, u32[]{:S(2)}, u32[]{:S(2)}) collective-permute-start(bf16[2,128,128]{2,1,0:T(8,128)(2,1)S(1)} %get-tuple-element.38), channel_id=1, source_target_pairs={{0,64},{64,128},{128,192},{192,0},{8,72},{72,136},{136,200},{200,8... | collective-permute-start | bytes 196616 | tf_op jit(solution)/shard_map/ppermute | solution.py:47
  76.2 5.3 %collective-permute-start.19 = (bf16[8,128,128]{2,1,0:T(8,128)(2,1)S(1)}, bf16[8,128,128]{2,1,0:T(8,128)(2,1)S(1)}, u32[]{:S(2)}, u32[]{:S(2)}) collective-permute-start(bf16[8,128,128]{2,1,0:T(8,128)(2,1)S(1)} %constant_dynamic-update-slice_fusion.2.refs_9_), channel_id=1, source_target_pairs={{0,56},{8,0},{16,8},{24,16},{32,24},{40,32},{48,40},{56,48},{64,12... | collective-permute-start | bytes 786440 | tf_op jit(solution)/shard_map/ppermute | solution.py:47
  77.0 6.4 %collective-permute-start.18 = (bf16[8,128,128]{2,1,0:T(8,128)(2,1)S(1)}, bf16[8,128,128]{2,1,0:T(8,128)(2,1)S(1)}, u32[]{:S(2)}, u32[]{:S(2)}) collective-permute-start(bf16[8,128,128]{2,1,0:T(8,128)(2,1)S(1)} %constant_dynamic-update-slice_fusion.2.refs_9_), channel_id=1, source_target_pairs={{0,8},{8,16},{16,24},{24,32},{32,40},{40,48},{48,56},{56,0},{64,72... | collective-permute-start | bytes 786440 | tf_op jit(solution)/shard_map/ppermute | solution.py:47
  81.5 5.8 %collective-permute-start.21 = (bf16[8,128,128]{2,1,0:T(8,128)(2,1)S(1)}, bf16[8,128,128]{2,1,0:T(8,128)(2,1)S(1)}, u32[]{:S(2)}, u32[]{:S(2)}) collective-permute-start(bf16[8,128,128]{2,1,0:T(8,128)(2,1)S(1)} %collective-permute-done.19.refs_11_), channel_id=1, source_target_pairs={{0,56},{8,0},{16,8},{24,16},{32,24},{40,32},{48,40},{56,48},{64,12... | collective-permute-start | bytes 786440 | tf_op jit(solution)/shard_map/ppermute | solution.py:47
  83.4 6.4 %collective-permute-start.20 = (bf16[8,128,128]{2,1,0:T(8,128)(2,1)S(1)}, bf16[8,128,128]{2,1,0:T(8,128)(2,1)S(1)}, u32[]{:S(2)}, u32[]{:S(2)}) collective-permute-start(bf16[8,128,128]{2,1,0:T(8,128)(2,1)S(1)} %collective-permute-done.18.refs_10_), channel_id=1, source_target_pairs={{0,8},{8,16},{16,24},{24,32},{32,40},{40,48},{48,56},{56,0},{64,72... | collective-permute-start | bytes 786440 | tf_op jit(solution)/shard_map/ppermute | solution.py:47
  87.3 7.2 %collective-permute-start.23 = (bf16[8,128,128]{2,1,0:T(8,128)(2,1)S(1)}, bf16[8,128,128]{2,1,0:T(8,128)(2,1)S(1)}, u32[]{:S(2)}, u32[]{:S(2)}) collective-permute-start(bf16[8,128,128]{2,1,0:T(8,128)(2,1)S(1)} %collective-permute-done.21.refs_13_), channel_id=1, source_target_pairs={{0,56},{8,0},{16,8},{24,16},{32,24},{40,32},{48,40},{56,48},{64,12... | collective-permute-start | bytes 786440 | tf_op jit(solution)/shard_map/ppermute | solution.py:47
  89.9 7.2 %collective-permute-start.22 = (bf16[8,128,128]{2,1,0:T(8,128)(2,1)S(1)}, bf16[8,128,128]{2,1,0:T(8,128)(2,1)S(1)}, u32[]{:S(2)}, u32[]{:S(2)}) collective-permute-start(bf16[8,128,128]{2,1,0:T(8,128)(2,1)S(1)} %collective-permute-done.20.refs_12_), channel_id=1, source_target_pairs={{0,8},{8,16},{16,24},{24,32},{32,40},{40,48},{48,56},{56,0},{64,72... | collective-permute-start | bytes 786440 | tf_op jit(solution)/shard_map/ppermute | solution.py:47
  94.5 5.7 %collective-permute-start.25 = (bf16[4,128,128]{2,1,0:T(8,128)(2,1)S(1)}, bf16[4,128,128]{2,1,0:T(8,128)(2,1)S(1)}, u32[]{:S(2)}, u32[]{:S(2)}) collective-permute-start(bf16[4,128,128]{2,1,0:T(8,128)(2,1)S(1)} %slice.27), channel_id=1, source_target_pairs={{0,56},{8,0},{16,8},{24,16},{32,24},{40,32},{48,40},{56,48},{64,12... | collective-permute-start | bytes 393224 | tf_op jit(solution)/shard_map/ppermute | solution.py:47
  97.1 7.1 %collective-permute-start.24 = (bf16[4,128,128]{2,1,0:T(8,128)(2,1)S(1)}, bf16[4,128,128]{2,1,0:T(8,128)(2,1)S(1)}, u32[]{:S(2)}, u32[]{:S(2)}) collective-permute-start(bf16[4,128,128]{2,1,0:T(8,128)(2,1)S(1)} %slice.26), channel_id=1, source_target_pairs={{0,8},{8,16},{16,24},{24,32},{32,40},{40,48},{48,56},{56,0},{64,72... | collective-permute-start | bytes 393224 | tf_op jit(solution)/shard_map/ppermute | solution.py:47
  116.2 8.6 %collective-permute-start.26 = (bf16[8,176,128]{2,1,0:T(8,128)(2,1)}, bf16[8,176,128]{2,1,0:T(8,128)(2,1)S(1)}, u32[]{:S(2)}, u32[]{:S(2)}) collective-permute-start(bf16[8,176,128]{2,1,0:T(8,128)(2,1)} %get-tuple-element.40), channel_id=1, source_target_pairs={{0,1},{1,0},{2,3},{3,2},{4,5},{5,4},{6,7},{7,6},{8,9},{9,8},{10,11... | collective-permute-start | bytes 1081352 | tf_op jit(solution)/shard_map/ppermute | solution.py:86
  125.9 5.4 %collective-permute-start.27 = (bf16[2,176,128]{2,1,0:T(8,128)(2,1)S(1)}, bf16[2,176,128]{2,1,0:T(8,128)(2,1)S(1)}, u32[]{:S(2)}, u32[]{:S(2)}) collective-permute-start(bf16[2,176,128]{2,1,0:T(8,128)(2,1)S(1)} %get-tuple-element.42), channel_id=1, source_target_pairs={{0,2},{1,3},{2,4},{3,5},{4,6},{5,7},{6,0},{7,1},{8,10},{9,11},{10,... | collective-permute-start | bytes 270344 | tf_op jit(solution)/shard_map/ppermute | solution.py:90
  127.1 6.6 %collective-permute-start.28 = (bf16[2,176,128]{2,1,0:T(8,128)(2,1)S(1)}, bf16[2,176,128]{2,1,0:T(8,128)(2,1)S(1)}, u32[]{:S(2)}, u32[]{:S(2)}) collective-permute-start(bf16[2,176,128]{2,1,0:T(8,128)(2,1)S(1)} %get-tuple-element.43), channel_id=1, source_target_pairs={{0,4},{1,5},{2,6},{3,7},{4,0},{5,1},{6,2},{7,3},{8,12},{9,13},{10,... | collective-permute-start | bytes 270344 | tf_op jit(solution)/shard_map/ppermute | solution.py:90
  129.3 4.6 %collective-permute-start.29 = (bf16[2,176,128]{2,1,0:T(8,128)(2,1)S(1)}, bf16[2,176,128]{2,1,0:T(8,128)(2,1)S(1)}, u32[]{:S(2)}, u32[]{:S(2)}) collective-permute-start(bf16[2,176,128]{2,1,0:T(8,128)(2,1)S(1)} %get-tuple-element.44), channel_id=1, source_target_pairs={{0,6},{1,7},{2,0},{3,1},{4,2},{5,3},{6,4},{7,5},{8,14},{9,15},{10,... | collective-permute-start | bytes 270344 | tf_op jit(solution)/shard_map/ppermute | solution.py:90
  139.4 7.6 %collective-permute-start.33 = (bf16[4,176,128]{2,1,0:T(8,128)(2,1)S(1)}, bf16[4,176,128]{2,1,0:T(8,128)(2,1)S(1)}, u32[]{:S(2)}, u32[]{:S(2)}) collective-permute-start(bf16[4,176,128]{2,1,0:T(8,128)(2,1)S(1)} %constant_dynamic-update-slice_fusion.6.w0), channel_id=1, source_target_pairs={{0,4},{1,5},{2,6},{3,7},{4,0},{5,1},{6,2},{7,3},{8,12},{9,13},{10,... | collective-permute-start | bytes 540680 | tf_op jit(solution)/shard_map/ppermute | solution.py:90
  142.6 8.8 %collective-permute-start.32 = (bf16[4,176,128]{2,1,0:T(8,128)(2,1)S(1)}, bf16[4,176,128]{2,1,0:T(8,128)(2,1)S(1)}, u32[]{:S(2)}, u32[]{:S(2)}) collective-permute-start(bf16[4,176,128]{2,1,0:T(8,128)(2,1)S(1)} %constant_dynamic-update-slice_fusion.6.w0), channel_id=1, source_target_pairs={{0,6},{1,7},{2,0},{3,1},{4,2},{5,3},{6,4},{7,5},{8,14},{9,15},{10,... | collective-permute-start | bytes 540680 | tf_op jit(solution)/shard_map/ppermute | solution.py:90
  143.4 8.0 %collective-permute-start.31 = (bf16[4,176,128]{2,1,0:T(8,128)(2,1)S(1)}, bf16[4,176,128]{2,1,0:T(8,128)(2,1)S(1)}, u32[]{:S(2)}, u32[]{:S(2)}) collective-permute-start(bf16[4,176,128]{2,1,0:T(8,128)(2,1)S(1)} %constant_dynamic-update-slice_fusion.6.w0), channel_id=1, source_target_pairs={{0,2},{1,3},{2,4},{3,5},{4,6},{5,7},{6,0},{7,1},{8,10},{9,11},{10,... | collective-permute-start | bytes 540680 | tf_op jit(solution)/shard_map/ppermute | solution.py:90
  (40 other events, 499.9 us)
where the time goes:
time: 208 us; the launch traced here: 207 us
  starting transfers between devices  62.3 us (30%)
  Pallas kernels  49.7 us (24%)
  waiting for transfers between devices  48.6 us (23%)
  blocking collectives  35.3 us (17%)
  local copies, waits for them, and re-layouts  7.76 us (4%)
  other arithmetic  2.1 us (1%)
    ppermute x22, starting transfers between devices, step(): return lax.ppermute(x, 'row', pairs)  29.6 us
    ppermute x22, waiting for transfers between devices, step(): return lax.ppermute(x, 'row', pairs)  28.6 us
    all_to_all x2, blocking collectives, sum_everywhere(): x = lax.all_to_all(x, every, 0, 0, tiled=True, axis_index_groups=groups)  24.6 us
    ppermute x4, starting transfers between devices, to_sibling(): return lax.ppermute(x, 'col', [(i, i ^ 1) for i in range(8)])  17.8 us
    pallas_call x4, Pallas kernels, on_device(): call(functools.partial(degree_kernel, i * GROUP), shape((16, 8, EDGE), F3...  14.9 us
    ppermute x9, waiting for transfers between devices, along_x(): return lax.ppermute(x, 'col', [(i, (i + 2 * shift) % 8) for i in range(8)])  14.9 us
    pallas_call x1, Pallas kernels, on_device(): call(functools.partial(last_kernel, n_feat), shape((1280, EDGE), BF16), [...  14.9 us
    ppermute x9, starting transfers between devices, along_x(): return lax.ppermute(x, 'col', [(i, (i + 2 * shift) % 8) for i in range(8)])  14.9 us
  transfers between devices with their start and end apart: 35, of which 21 were waited for; matrix products, arithmetic and copies ran while one was open for 1% of the time, Pallas kernels for 7%

commit v1 on v0

--- a/solution.py
+++ b/solution.py
@@ -16,7 +16,6 @@
 VMEM = pl.BlockSpec(memory_space=pltpu.VMEM)
 SMEM = pl.BlockSpec(memory_space=pltpu.SMEM)
 ANY = pl.BlockSpec(memory_space=pl.ANY)
-HBM = pl.BlockSpec(memory_space=pltpu.HBM)
 NT = (((1,), (1,)), ((), ()))
 
 
@@ -112,42 +111,22 @@
     return copies
 
 
-def start_tiles(tiles, held, sems):
-    copies = []
-    for i in range(held.shape[0] // GROUP):
-        at = pl.ds(i * GROUP, GROUP)
-        copies.append(pltpu.make_async_copy(tiles.at[at], held.at[at], sems.at[i]))
-        copies[-1].start()
-    return copies
-
-
-def start_all(pairs, sems):
-    copies = [pltpu.make_async_copy(a, b, sems.at[i]) for i, (a, b) in enumerate(pairs)]
-    for c in copies:
-        c.start()
-    return copies
-
-
-def accumulate(tiles, held, sems, product, add):
+def accumulate(count, product, add):
     def body(i, carry):
-        at = pl.ds(i * GROUP, GROUP)
-        pltpu.make_async_copy(tiles.at[at], held.at[at], sems.at[i]).wait()
         got = [product(i * GROUP + u) for u in range(GROUP)]
         for u in range(GROUP):
             add(i * GROUP + u, got[u])
         return carry
 
-    lax.fori_loop(0, held.shape[0] // GROUP, body, 0)
-
-
-def degree_kernel(first, slots, tiles, out, held, sem):
-    tiles = tiles.at[pl.ds(first, GROUP)]
-    start_tiles(tiles, held, sem)
+    lax.fori_loop(0, count // GROUP, body, 0)
+
+
+def degree_kernel(first, slots, tiles, out):
     out[...] = jnp.zeros_like(out)
     ones = jnp.ones((8, EDGE), BF16)
 
     def product(t):
-        x = held[t].astype(F32)
+        x = tiles[first + t].astype(F32)
         x = x * x
         hi = x.astype(BF16)
         lo = (x - hi.astype(F32)).astype(BF16)
@@ -156,13 +135,12 @@
     def add(t, got):
         out[slots[first + t]] += got
 
-    accumulate(tiles, held, sem, product, add)
-
-
-def first_kernel(n_parts, offs, cols, tiles_hbm, d0, d1, d2, d3, *refs):
-    parts, keep, send, tiles, held, acc, tile_sem, sem = refs[:n_parts], *refs[n_parts:]
+    accumulate(GROUP, product, add)
+
+
+def first_kernel(n_parts, offs, cols, tiles, d0, d1, d2, d3, *refs):
+    parts, keep, send, held, acc, sem = refs[:n_parts], *refs[n_parts:]
     copies = start_parts(parts, held, sem)
-    start_tiles(tiles_hbm, tiles, tile_sem)
     acc[...] = jnp.zeros_like(acc)
     for s in range(16):
         deg = (d0[s][:1] + d1[s][:1]) + (d2[s][:1] + d3[s][:1])
@@ -173,7 +151,7 @@
     def add(t, got):
         acc[pl.ds(pl.multiple_of(offs[t], 8), EDGE), :] += got
 
-    accumulate(tiles_hbm, tiles, tile_sem, lambda t: dot(tiles[t], held[cols[t]]), add)
+    accumulate(tiles.shape[0], lambda t: dot(tiles[t], held[cols[t]]), add)
     keep[...] = acc[pl.ds(0, 1056), :]
     send[...] = acc[pl.ds(1056, 1056), :]
 
@@ -207,13 +185,10 @@
         agg[b] = (column * total[b * EDGE : (b + 1) * EDGE]).astype(BF16)
 
 
-def second_kernel(n_parts, slots, cols, tiles_hbm, neigh_hbm, weights, bias, *refs):
+def second_kernel(n_parts, slots, cols, tiles, neigh, weights, bias, *refs):
     feat_parts, agg_parts = refs[:n_parts], refs[n_parts : 2 * n_parts]
-    agg, keep, send, mine, tiles, neigh, both, held, acc, tile_sem, sem, neigh_sem = refs[2 * n_parts :]
+    agg, keep, send, mine, both, held, acc, sem = refs[2 * n_parts :]
     copies = start_pairs(feat_parts, agg_parts, both, sem)
-    start_tiles(tiles_hbm, tiles, tile_sem)
-    neigh_copy = pltpu.make_async_copy(neigh_hbm, neigh, neigh_sem)
-    neigh_copy.start()
     acc[...] = jnp.zeros_like(acc)
     weights_t = flip(weights[...]).astype(BF16)
     wide = 4
@@ -234,8 +209,7 @@
     def add(t, got):
         acc[slots[t]] += got
 
-    accumulate(tiles_hbm, tiles, tile_sem, lambda t: dot_nt(held[cols[t]], tiles[t]), add)
-    neigh_copy.wait()
+    accumulate(tiles.shape[0], lambda t: dot_nt(held[cols[t]], tiles[t]), add)
     for s in range(16):
         agg[s] = acc[s].astype(BF16)
         got = dot(neigh[pl.ds(0, PAD), :], agg[s]).astype(BF16)
@@ -278,28 +252,14 @@
 
 
 def last_kernel(
-    n_parts, slots, cols, w0, w1, w2, w3, weights, bias, tiles_hbm, agg_second_hbm, lg_hbm, self_hbm,
-    neigh_hbm, grad_self_hbm, grad_bias, *refs
+    n_parts, slots, cols, w0, w1, w2, w3, weights, bias, tiles, agg_second, lg, self_t, neigh_t,
+    grad_self, grad_bias, *refs
 ):
     feat_parts, agg_parts = refs[:n_parts], refs[n_parts : 2 * n_parts]
-    (
-        out, tiles, agg_second, lg, self_t, neigh_t, grad_self, both, acc, proj,
-        tile_sem, both_sem, sems,
-    ) = refs[2 * n_parts :]
-    pairs = (
-        (neigh_hbm, neigh_t),
-        (agg_second_hbm, agg_second),
-        (lg_hbm, lg),
-        (self_hbm, self_t),
-        (grad_self_hbm, grad_self),
-    )
-    small = start_all(pairs, sems)
-    start_tiles(tiles_hbm, tiles, tile_sem)
+    out, both, acc, proj, both_sem = refs[2 * n_parts :]
     copies = start_pairs(feat_parts, agg_parts, both, both_sem)
     acc[...] = jnp.zeros_like(acc)
     weights_t = flip(weights[...]).astype(BF16)
-    for c in small:
-        c.wait()
     lacking = jnp.zeros((256 - PAD, EDGE), BF16)
     self_second = flip(self_t[...]).astype(BF16)
     neigh_second = flip(neigh_t[...]).astype(BF16)
@@ -322,7 +282,7 @@
     def add(t, got):
         acc[cols[t]] += got
 
-    accumulate(tiles_hbm, tiles, tile_sem, lambda t: dot(proj[slots[t]], tiles[t]), add)
+    accumulate(tiles.shape[0], lambda t: dot(proj[slots[t]], tiles[t]), add)
     for c in copies:
         c.wait()
     wide = 8
@@ -420,7 +380,6 @@
     shape = jax.ShapeDtypeStruct
     dma = pltpu.SemaphoreType.DMA
     feat = features.reshape(2, EDGE, EDGE)
-    tile_buffer = pltpu.VMEM(tiles.shape, BF16)
     n_groups = tiles.shape[0] // GROUP
 
     feat_parts = ring(jnp.concatenate(along_y(feat), axis=0), ALONG_Z)
@@ -429,9 +388,8 @@
         call(
             functools.partial(degree_kernel, i * GROUP),
             shape((16, 8, EDGE), F32),
-            [SMEM, HBM],
-            [pltpu.VMEM((GROUP, EDGE, EDGE), BF16), dma((1,))],
-            mib=60,
+            [SMEM, VMEM],
+            mib=4,
             flops=2**32,
             bytes_accessed=2**20,
         )(slots, tiles)
@@ -441,15 +399,13 @@
     keep, send = call(
         functools.partial(first_kernel, n_feat),
         (block, block),
-        [SMEM, SMEM, HBM] + [VMEM] * 4 + [ANY] * n_feat,
+        [SMEM] * 2 + [VMEM] * 5 + [ANY] * n_feat,
         [
-            tile_buffer,
             pltpu.VMEM((64, EDGE, EDGE), BF16),
             pltpu.VMEM((2112, EDGE), F32),
-            dma((n_groups,)),
             dma((n_feat,)),
         ],
-        mib=60,
+        mib=8,
         flops=2**29,
         bytes_accessed=2**23,
     )(offs, cols, tiles, *degs, *feat_parts)
@@ -471,18 +427,14 @@
     agg_second, keep, send, hid = call(
         functools.partial(second_kernel, n_feat),
         (shape((16, hid_size, EDGE), BF16), half, half, shape((2, hid_size, EDGE), BF16)),
-        [SMEM, SMEM, HBM, HBM, VMEM, VMEM] + [HBM] * (2 * n_feat),
+        [SMEM] * 2 + [VMEM] * 4 + [ANY] * (2 * n_feat),
         [
-            tile_buffer,
-            pltpu.VMEM((256, hid_size), BF16),
             pltpu.VMEM((64, EDGE, 2 * EDGE), BF16),
             pltpu.VMEM((64, hid_size, EDGE), BF16),
             pltpu.VMEM((16, hid_size, EDGE), F32),
-            dma((n_groups,)),
             dma((2 * n_feat,)),
-            dma(()),
         ],
-        mib=60,
+        mib=18,
         flops=2**31,
         bytes_accessed=2**23,
     )(slots, cols, tiles, neigh_t, weights, bias, *feat_parts, *agg_parts)
@@ -515,22 +467,14 @@
     grads = call(
         functools.partial(last_kernel, n_feat),
         shape((1280, EDGE), BF16),
-        [SMEM] * 2 + [VMEM] * 6 + [HBM] * 6 + [VMEM] + [HBM] * (2 * n_feat),
+        [SMEM] * 2 + [VMEM] * 13 + [ANY] * (2 * n_feat),
         [
-            tile_buffer,
-            pltpu.VMEM((16, hid_size, EDGE), BF16),
-            pltpu.VMEM((2, PAD, EDGE), BF16),
-            pltpu.VMEM((256, hid_size), BF16),
-            pltpu.VMEM((256, hid_size), BF16),
-            pltpu.VMEM((PAD, hid_size), F32),
             pltpu.VMEM((64, EDGE, 2 * EDGE), BF16),
             pltpu.VMEM((64, hid_size, EDGE), F32),
             pltpu.VMEM((16, hid_size, EDGE), BF16),
-            dma((n_groups,)),
             dma((2 * n_feat,)),
-            dma((5,)),
         ],
-        mib=60,
+        mib=22,
         flops=2**31,
         bytes_accessed=2**24,
     )(

time: 208 us -> 201 us (0.966); the launches traced: 207 us -> 197 us
  Pallas kernels: 49.7 us -> 31 us
  starting transfers between devices: 62.3 us -> 72.6 us
  local copies, waits for them, and re-layouts: 7.76 us -> 2.47 us
  waiting for transfers between devices: 48.6 us -> 52.7 us
    ppermute x22, starting transfers between devices: 29.6 us -> 40 us  [step(): return lax.ppermute(x, 'row', pairs)]
    pallas_call x4, Pallas kernels: 14.9 us -> 6.89 us  [on_device(): call(functools.partial(degree_kernel, i * GROUP), shape((16, 8, EDGE), F3...]
    unnamed x79 -> x25, local copies, waits for them, and re-layouts: 6.9 us -> 2.27 us
    ppermute x22, waiting for transfers between devices: 28.6 us -> 32.9 us  [step(): return lax.ppermute(x, 'row', pairs)]
    pallas_call x1, Pallas kernels: 14.9 us -> 10.9 us  [on_device(): call(functools.partial(last_kernel, n_feat), shape((1280, EDGE), BF16), [...]
    pallas_call x1, Pallas kernels: 11.4 us -> 8.05 us  [on_device(): call(functools.partial(second_kernel, n_feat), (shape((16, hid_size, EDGE...]
    pallas_call x1, Pallas kernels: 6.53 us -> 3.25 us  [on_device(): call(functools.partial(first_kernel, n_feat), (block, block), [SMEM] * 2...]
  transfers between devices with their start and end apart: 35 -> 35, of which waited for: 21 -> 22; matrix products, arithmetic and copies ran while one was open for 1% -> 0% of each run, Pallas kernels for 7% -> 3%
where the time goes in v1:
time: 201 us; the launch traced here: 197 us
  starting transfers between devices  72.6 us (36%)
  waiting for transfers between devices  52.7 us (26%)
  blocking collectives  35.5 us (18%)
  Pallas kernels  31 us (15%)
  local copies, waits for them, and re-layouts  2.47 us (1%)
    ppermute x22, starting transfers between devices, step(): return lax.ppermute(x, 'row', pairs)  40 us
    ppermute x22, waiting for transfers between devices, step(): return lax.ppermute(x, 'row', pairs)  32.9 us
    all_to_all x2, blocking collectives, sum_everywhere(): x = lax.all_to_all(x, every, 0, 0, tiled=True, axis_index_groups=groups)  24.8 us
    ppermute x4, starting transfers between devices, to_sibling(): return lax.ppermute(x, 'col', [(i, i ^ 1) for i in range(8)])  18.3 us
    ppermute x9, waiting for transfers between devices, along_x(): return lax.ppermute(x, 'col', [(i, (i + 2 * shift) % 8) for i in range(8)])  15.1 us
    ppermute x9, starting transfers between devices, along_x(): return lax.ppermute(x, 'col', [(i, (i + 2 * shift) % 8) for i in range(8)])  14.3 us
    pallas_call x1, Pallas kernels, on_device(): call(functools.partial(last_kernel, n_feat), shape((1280, EDGE), BF16), [...  10.9 us
    all_to_all x1, blocking collectives, sum_everywhere(): x = lax.all_to_all(x, 'row', 0, 0, tiled=True, axis_index_groups=ALONG_Z)  10.8 us
  transfers between devices with their start and end apart: 35, of which 22 were waited for; matrix products, arithmetic and copies ran while one was open for 0% of the time, Pallas kernels for 3%

profile of v1, /device:TPU:1, one launch (start us, length us, event | category | flops | bytes accessed | tf_op | source)
XLA Modules:
  0.0 197.0 jit_solution(9679668104729997472)
XLA Ops:
  0.6 3.8 %collective-permute-start.2 = (bf16[2,128,128]{2,1,0:T(8,128)(2,1)}, bf16[2,128,128]{2,1,0:T(8,128)(2,1)S(1)}, u32[]{:S(2)}, u32[]{:S(2)}) collective-permute-start(bf16[2,128,128]{2,1,0:T(8,128)(2,1)} %bitcast.56), channel_id=1, source_target_pairs={{0,128},{64,192},{128,0},{192,64},{8,136},{72,200},{136,8},{200,72... | collective-permute-start | bytes 196616 | tf_op jit(solution)/shard_map/ppermute | solution.py:46
  6.7 2.1 %collective-permute-done.1 = bf16[2,128,128]{2,1,0:T(8,128)(2,1)S(1)} collective-permute-done((bf16[2,128,128]{2,1,0:T(8,128)(2,1)}, bf16[2,128,128]{2,1,0:T(8,128)(2,1)S(1)}, u32[]{:S(2)}, u32[]{:S(2)}) %collective-permute-start.1) | collective-permute-done | bytes 65568 | tf_op jit(solution)/shard_map/ppermute | solution.py:46
  10.8 5.5 %collective-permute-start.4 = (bf16[8,128,128]{2,1,0:T(8,128)(2,1)S(1)}, bf16[8,128,128]{2,1,0:T(8,128)(2,1)S(1)}, u32[]{:S(2)}, u32[]{:S(2)}) collective-permute-start(bf16[8,128,128]{2,1,0:T(8,128)(2,1)S(1)} %pad_maximum_fusion.refs_0_), channel_id=1, source_target_pairs={{0,56},{8,0},{16,8},{24,16},{32,24},{40,32},{48,40},{56,48},{64,12... | collective-permute-start | bytes 786440 | tf_op jit(solution)/shard_map/ppermute | solution.py:46
  16.3 2.2 %copy-done = bf16[1,1,128,128,128]{4,3,2,1,0:T(8,128)(2,1)S(1)} copy-done((bf16[1,1,128,128,128]{4,3,2,1,0:T(8,128)(2,1)S(1)}, bf16[1,1,128,128,128]{4,3,2,1,0:T(8,128)(2,1)}, u32[]{:S(2)}) %copy-start) | copy-done | bytes 4194328
  20.2 2.8 %collective-permute-start.6 = (bf16[8,128,128]{2,1,0:T(8,128)(2,1)S(1)}, bf16[8,128,128]{2,1,0:T(8,128)(2,1)S(1)}, u32[]{:S(2)}, u32[]{:S(2)}) collective-permute-start(bf16[8,128,128]{2,1,0:T(8,128)(2,1)S(1)} %collective-permute-done.4.refs_2_), channel_id=1, source_target_pairs={{0,56},{8,0},{16,8},{24,16},{32,24},{40,32},{48,40},{56,48},{64,12... | collective-permute-start | bytes 786440 | tf_op jit(solution)/shard_map/ppermute | solution.py:46
  26.3 3.1 %collective-permute-start.8 = (bf16[8,128,128]{2,1,0:T(8,128)(2,1)S(1)}, bf16[8,128,128]{2,1,0:T(8,128)(2,1)S(1)}, u32[]{:S(2)}, u32[]{:S(2)}) collective-permute-start(bf16[8,128,128]{2,1,0:T(8,128)(2,1)S(1)} %collective-permute-done.6.refs_4_), channel_id=1, source_target_pairs={{0,56},{8,0},{16,8},{24,16},{32,24},{40,32},{48,40},{56,48},{64,12... | collective-permute-start | bytes 786440 | tf_op jit(solution)/shard_map/ppermute | solution.py:46
  32.9 3.2 %collective-permute-start.10 = (bf16[4,128,128]{2,1,0:T(8,128)(2,1)S(1)}, bf16[4,128,128]{2,1,0:T(8,128)(2,1)S(1)}, u32[]{:S(2)}, u32[]{:S(2)}) collective-permute-start(bf16[4,128,128]{2,1,0:T(8,128)(2,1)S(1)} %slice.25), channel_id=1, source_target_pairs={{0,56},{8,0},{16,8},{24,16},{32,24},{40,32},{48,40},{56,48},{64,12... | collective-permute-start | bytes 393224 | tf_op jit(solution)/shard_map/ppermute | solution.py:46
  39.1 3.7 %collective-permute-done.9.refs_7_ = bf16[4,128,128]{2,1,0:T(8,128)(2,1)S(1)} collective-permute-done((bf16[4,128,128]{2,1,0:T(8,128)(2,1)S(1)}, bf16[4,128,128]{2,1,0:T(8,128)(2,1)S(1)}, u32[]{:S(2)}, u32[]{:S(2)}) %collective-permute-start.9) | collective-permute-done | bytes 131104 | tf_op jit(solution)/shard_map/ppermute | solution.py:46
  42.8 3.3 %shard_map.167 = (f32[1056,128]{1,0:T(8,128)S(1)}, f32[1056,128]{1,0:T(8,128)S(1)}) custom-call(s32[128]{0:T(128)S(1)} %get-tuple-element.58.offs, s32[128]{0:T(128)S(1)} %get-tuple-element.60.cols, bf16[128,128,128]{2,1,0:T(8,128)(2,1)S(1)} %bitcast.45, f32[16,8,128]{2,1,0:T(8,128)S(1)} %shard_map.163.d0, f32[16,8,128]{2,1,0:T(8,128)S(1)} %shard_map.164.d1, ...), custom_call_target="tpu_custom_call" | custom-call | flops 536870912 | bytes 8388608 | tf_op jit(solution)/shard_map/pallas_call | solution.py:399
  46.0 7.0 %collective-permute-start.11 = (f32[1056,128]{1,0:T(8,128)S(1)}, f32[1056,128]{1,0:T(8,128)S(1)}, u32[]{:S(2)}, u32[]{:S(2)}) collective-permute-start(f32[1056,128]{1,0:T(8,128)S(1)} %get-tuple-element.33), channel_id=1, source_target_pairs={{0,1},{1,0},{2,3},{3,2},{4,5},{5,4},{6,7},{7,6},{8,9},{9,8},{10,11... | collective-permute-start | bytes 1622024 | tf_op jit(solution)/shard_map/ppermute | solution.py:85
  55.9 2.4 %collective-permute-start.13 = (f32[264,128]{1,0:T(8,128)S(1)}, f32[264,128]{1,0:T(8,128)S(1)}, u32[]{:S(2)}, u32[]{:S(2)}) collective-permute-start(f32[264,128]{1,0:T(8,128)S(1)} %get-tuple-element.36), channel_id=1, source_target_pairs={{0,4},{1,5},{2,6},{3,7},{4,0},{5,1},{6,2},{7,3},{8,12},{9,13},{10,... | collective-permute-start | bytes 405512 | tf_op jit(solution)/shard_map/ppermute | solution.py:89
  60.7 3.9 %collective-permute-done.13.s2 = f32[264,128]{1,0:T(8,128)S(1)} collective-permute-done((f32[264,128]{1,0:T(8,128)S(1)}, f32[264,128]{1,0:T(8,128)S(1)}, u32[]{:S(2)}, u32[]{:S(2)}) %collective-permute-start.13) | collective-permute-done | bytes 135200 | tf_op jit(solution)/shard_map/ppermute | solution.py:89
  66.5 5.0 %collective-permute-done.15 = bf16[2,128,128]{2,1,0:T(8,128)(2,1)S(1)} collective-permute-done((bf16[2,128,128]{2,1,0:T(8,128)(2,1)S(1)}, bf16[2,128,128]{2,1,0:T(8,128)(2,1)S(1)}, u32[]{:S(2)}, u32[]{:S(2)}) %collective-permute-start.15) | collective-permute-done | bytes 65568 | tf_op jit(solution)/shard_map/ppermute | solution.py:46
  73.1 4.1 %collective-permute-done.19.refs_11_ = bf16[8,128,128]{2,1,0:T(8,128)(2,1)S(1)} collective-permute-done((bf16[8,128,128]{2,1,0:T(8,128)(2,1)S(1)}, bf16[8,128,128]{2,1,0:T(8,128)(2,1)S(1)}, u32[]{:S(2)}, u32[]{:S(2)}) %collective-permute-start.19) | collective-permute-done | bytes 262176 | tf_op jit(solution)/shard_map/ppermute | solution.py:46
  78.8 3.7 %collective-permute-done.21.refs_13_ = bf16[8,128,128]{2,1,0:T(8,128)(2,1)S(1)} collective-permute-done((bf16[8,128,128]{2,1,0:T(8,128)(2,1)S(1)}, bf16[8,128,128]{2,1,0:T(8,128)(2,1)S(1)}, u32[]{:S(2)}, u32[]{:S(2)}) %collective-permute-start.21) | collective-permute-done | bytes 262176 | tf_op jit(solution)/shard_map/ppermute | solution.py:46
  82.5 2.7 %collective-permute-start.23 = (bf16[8,128,128]{2,1,0:T(8,128)(2,1)S(1)}, bf16[8,128,128]{2,1,0:T(8,128)(2,1)S(1)}, u32[]{:S(2)}, u32[]{:S(2)}) collective-permute-start(bf16[8,128,128]{2,1,0:T(8,128)(2,1)S(1)} %collective-permute-done.21.refs_13_), channel_id=1, source_target_pairs={{0,56},{8,0},{16,8},{24,16},{32,24},{40,32},{48,40},{56,48},{64,12... | collective-permute-start | bytes 786440 | tf_op jit(solution)/shard_map/ppermute | solution.py:46
  85.2 3.9 %collective-permute-done.23.refs_15_ = bf16[8,128,128]{2,1,0:T(8,128)(2,1)S(1)} collective-permute-done((bf16[8,128,128]{2,1,0:T(8,128)(2,1)S(1)}, bf16[8,128,128]{2,1,0:T(8,128)(2,1)S(1)}, u32[]{:S(2)}, u32[]{:S(2)}) %collective-permute-start.23) | collective-permute-done | bytes 262176 | tf_op jit(solution)/shard_map/ppermute | solution.py:46
  89.1 2.6 %collective-permute-start.25 = (bf16[4,128,128]{2,1,0:T(8,128)(2,1)S(1)}, bf16[4,128,128]{2,1,0:T(8,128)(2,1)S(1)}, u32[]{:S(2)}, u32[]{:S(2)}) collective-permute-start(bf16[4,128,128]{2,1,0:T(8,128)(2,1)S(1)} %slice.27), channel_id=1, source_target_pairs={{0,56},{8,0},{16,8},{24,16},{32,24},{40,32},{48,40},{56,48},{64,12... | collective-permute-start | bytes 393224 | tf_op jit(solution)/shard_map/ppermute | solution.py:46
  91.7 9.7 %collective-permute-start.24 = (bf16[4,128,128]{2,1,0:T(8,128)(2,1)S(1)}, bf16[4,128,128]{2,1,0:T(8,128)(2,1)S(1)}, u32[]{:S(2)}, u32[]{:S(2)}) collective-permute-start(bf16[4,128,128]{2,1,0:T(8,128)(2,1)S(1)} %slice.26), channel_id=1, source_target_pairs={{0,8},{8,16},{16,24},{24,32},{32,40},{40,48},{48,56},{56,0},{64,72... | collective-permute-start | bytes 393224 | tf_op jit(solution)/shard_map/ppermute | solution.py:46
  101.5 4.9 %collective-permute-done.24.refs_16_ = bf16[4,128,128]{2,1,0:T(8,128)(2,1)S(1)} collective-permute-done((bf16[4,128,128]{2,1,0:T(8,128)(2,1)S(1)}, bf16[4,128,128]{2,1,0:T(8,128)(2,1)S(1)}, u32[]{:S(2)}, u32[]{:S(2)}) %collective-permute-start.24) | collective-permute-done | bytes 131104 | tf_op jit(solution)/shard_map/ppermute | solution.py:46
  106.5 8.0 %shard_map.170 = (bf16[16,256,128]{2,1,0:T(8,128)(2,1)S(1)}, bf16[8,176,128]{2,1,0:T(8,128)(2,1)S(1)}, bf16[8,176,128]{2,1,0:T(8,128)(2,1)S(1)}, bf16[2,256,128]{2,1,0:T(8,128)(2,1)S(1)}) custom-call(s32[128]{0:T(128)S(1)} %get-tuple-element.59.slots, s32[128]{0:T(128)S(1)} %get-tuple-element.60.cols, bf16[128,128,128]{2,1,0:T(8,128)(2,1)S(1)} %bitcast.46, ...), custom_call_target="tpu_custom_call" | custom-call | flops 2147483648 | bytes 8388608 | tf_op jit(solution)/shard_map/pallas_call | solution.py:427
  114.5 7.3 %collective-permute-start.26 = (bf16[8,176,128]{2,1,0:T(8,128)(2,1)S(1)}, bf16[8,176,128]{2,1,0:T(8,128)(2,1)S(1)}, u32[]{:S(2)}, u32[]{:S(2)}) collective-permute-start(bf16[8,176,128]{2,1,0:T(8,128)(2,1)S(1)} %get-tuple-element.40), channel_id=1, source_target_pairs={{0,1},{1,0},{2,3},{3,2},{4,5},{5,4},{6,7},{7,6},{8,9},{9,8},{10,11... | collective-permute-start | bytes 1081352 | tf_op jit(solution)/shard_map/ppermute | solution.py:85
  124.4 2.1 %collective-permute-start.28 = (bf16[2,176,128]{2,1,0:T(8,128)(2,1)S(1)}, bf16[2,176,128]{2,1,0:T(8,128)(2,1)S(1)}, u32[]{:S(2)}, u32[]{:S(2)}) collective-permute-start(bf16[2,176,128]{2,1,0:T(8,128)(2,1)S(1)} %get-tuple-element.43), channel_id=1, source_target_pairs={{0,4},{1,5},{2,6},{3,7},{4,0},{5,1},{6,2},{7,3},{8,12},{9,13},{10,... | collective-permute-start | bytes 270344 | tf_op jit(solution)/shard_map/ppermute | solution.py:89
  128.4 2.4 %collective-permute-done.28.s2 = bf16[2,176,128]{2,1,0:T(8,128)(2,1)S(1)} collective-permute-done((bf16[2,176,128]{2,1,0:T(8,128)(2,1)S(1)}, bf16[2,176,128]{2,1,0:T(8,128)(2,1)S(1)}, u32[]{:S(2)}, u32[]{:S(2)}) %collective-permute-start.28) | collective-permute-done | bytes 90144 | tf_op jit(solution)/shard_map/ppermute | solution.py:89
  134.1 2.9 %collective-permute-start.33 = (bf16[4,176,128]{2,1,0:T(8,128)(2,1)S(1)}, bf16[4,176,128]{2,1,0:T(8,128)(2,1)S(1)}, u32[]{:S(2)}, u32[]{:S(2)}) collective-permute-start(bf16[4,176,128]{2,1,0:T(8,128)(2,1)S(1)} %constant_dynamic-update-slice_fusion.6.w0), channel_id=1, source_target_pairs={{0,4},{1,5},{2,6},{3,7},{4,0},{5,1},{6,2},{7,3},{8,12},{9,13},{10,... | collective-permute-start | bytes 540680 | tf_op jit(solution)/shard_map/ppermute | solution.py:89
  138.4 3.0 %collective-permute-done.33.w3 = bf16[4,176,128]{2,1,0:T(8,128)(2,1)S(1)} collective-permute-done((bf16[4,176,128]{2,1,0:T(8,128)(2,1)S(1)}, bf16[4,176,128]{2,1,0:T(8,128)(2,1)S(1)}, u32[]{:S(2)}, u32[]{:S(2)}) %collective-permute-start.33) | collective-permute-done | bytes 180256 | tf_op jit(solution)/shard_map/ppermute | solution.py:89
  141.4 4.3 %collective-permute-done.32.w2 = bf16[4,176,128]{2,1,0:T(8,128)(2,1)S(1)} collective-permute-done((bf16[4,176,128]{2,1,0:T(8,128)(2,1)S(1)}, bf16[4,176,128]{2,1,0:T(8,128)(2,1)S(1)}, u32[]{:S(2)}, u32[]{:S(2)}) %collective-permute-start.32) | collective-permute-done | bytes 180256 | tf_op jit(solution)/shard_map/ppermute | solution.py:89
  145.7 10.9 %shard_map.173 = bf16[1280,128]{1,0:T(8,128)(2,1)S(1)} custom-call(s32[128]{0:T(128)S(1)} %get-tuple-element.59.slots, s32[128]{0:T(128)S(1)} %get-tuple-element.60.cols, bf16[4,176,128]{2,1,0:T(8,128)(2,1)S(1)} %constant_dynamic-update-slice_fusion.6.w0, bf16[4,176,128]{2,1,0:T(8,128)(2,1)S(1)} %collective-permute-done.31.w1, ...), custom_call_target="tpu_custom_call" | custom-call | flops 2147483648 | bytes 16777216 | tf_op jit(solution)/shard_map/pallas_call | solution.py:467
  156.6 13.3 %all_to_all.15.x = bf16[16,80,128]{2,1,0:T(8,128)(2,1)S(1)} all-to-all(bf16[16,80,128]{2,1,0:T(8,128)(2,1)S(1)} %bitcast.48), channel_id=1, replica_groups={{0,2,4,6,64,66,68,70,128,130,132,134,192,194,196,198},{1,3,5,7,65,67,69..., dimensions={0} | all-to-all | bytes 655360 | tf_op jit(solution)/shard_map/all_to_all | solution.py:347
  170.0 10.8 %all_to_all.16.x = bf16[8,80,128]{2,1,0:T(8,128)(2,1)S(1)} all-to-all(bf16[8,80,128]{2,1,0:T(8,128)(2,1)S(1)} %broadcast_in_dim.9), channel_id=1, replica_groups={{0,8,16,24,32,40,48,56},{64,72,80,88,96,104,112,120},{128,136,144,152,1..., dimensions={0} | all-to-all | bytes 327680 | tf_op jit(solution)/shard_map/all_to_all | solution.py:350
  180.8 2.8 %collective-permute-start.34 = (bf16[80,128]{1,0:T(8,128)(2,1)S(1)}, bf16[80,128]{1,0:T(8,128)(2,1)S(1)}, u32[]{:S(2)}, u32[]{:S(2)}) collective-permute-start(bf16[80,128]{1,0:T(8,128)(2,1)S(1)} %shard_map.175.a), channel_id=1, source_target_pairs={{0,1},{1,0},{2,3},{3,2},{4,5},{5,4},{6,7},{7,6},{8,9},{9,8},{10,11... | collective-permute-start | bytes 61448 | tf_op jit(solution)/shard_map/ppermute | solution.py:85
  184.5 11.5 %all_to_all.17 = bf16[16,80,128]{2,1,0:T(8,128)(2,1)S(1)} all-to-all(bf16[16,80,128]{2,1,0:T(8,128)(2,1)S(1)} %shard_map.176), channel_id=1, replica_groups={{0,2,4,6,64,66,68,70,128,130,132,134,192,194,196,198},{1,3,5,7,65,67,69..., dimensions={0} | all-to-all | bytes 655360 | tf_op jit(solution)/shard_map/all_to_all | solution.py:353
  (95 shorter events, 37.0 us)
Async XLA Ops:
  0.6 6.0 %collective-permute-start.2 = (bf16[2,128,128]{2,1,0:T(8,128)(2,1)}, bf16[2,128,128]{2,1,0:T(8,128)(2,1)S(1)}, u32[]{:S(2)}, u32[]{:S(2)}) collective-permute-start(bf16[2,128,128]{2,1,0:T(8,128)(2,1)} %bitcast.56), channel_id=1, source_target_pairs={{0,128},{64,192},{128,0},{192,64},{8,136},{72,200},{136,8},{200,72... | collective-permute-start | bytes 196616 | tf_op jit(solution)/shard_map/ppermute | solution.py:46
  5.2 4.7 %collective-permute-start = (bf16[2,128,128]{2,1,0:T(8,128)(2,1)}, bf16[2,128,128]{2,1,0:T(8,128)(2,1)S(1)}, u32[]{:S(2)}, u32[]{:S(2)}) collective-permute-start(bf16[2,128,128]{2,1,0:T(8,128)(2,1)} %bitcast.58), channel_id=1, source_target_pairs={{0,64},{64,128},{128,192},{192,0},{8,72},{72,136},{136,200},{200,8... | collective-permute-start | bytes 196616 | tf_op jit(solution)/shard_map/ppermute | solution.py:46
  10.8 9.4 %collective-permute-start.4 = (bf16[8,128,128]{2,1,0:T(8,128)(2,1)S(1)}, bf16[8,128,128]{2,1,0:T(8,128)(2,1)S(1)}, u32[]{:S(2)}, u32[]{:S(2)}) collective-permute-start(bf16[8,128,128]{2,1,0:T(8,128)(2,1)S(1)} %pad_maximum_fusion.refs_0_), channel_id=1, source_target_pairs={{0,56},{8,0},{16,8},{24,16},{32,24},{40,32},{48,40},{56,48},{64,12... | collective-permute-start | bytes 786440 | tf_op jit(solution)/shard_map/ppermute | solution.py:46
  16.3 6.7 %collective-permute-start.3 = (bf16[8,128,128]{2,1,0:T(8,128)(2,1)S(1)}, bf16[8,128,128]{2,1,0:T(8,128)(2,1)S(1)}, u32[]{:S(2)}, u32[]{:S(2)}) collective-permute-start(bf16[8,128,128]{2,1,0:T(8,128)(2,1)S(1)} %pad_maximum_fusion.refs_0_), channel_id=1, source_target_pairs={{0,8},{8,16},{16,24},{24,32},{32,40},{40,48},{48,56},{56,0},{64,72... | collective-permute-start | bytes 786440 | tf_op jit(solution)/shard_map/ppermute | solution.py:46
  20.2 6.1 %collective-permute-start.6 = (bf16[8,128,128]{2,1,0:T(8,128)(2,1)S(1)}, bf16[8,128,128]{2,1,0:T(8,128)(2,1)S(1)}, u32[]{:S(2)}, u32[]{:S(2)}) collective-permute-start(bf16[8,128,128]{2,1,0:T(8,128)(2,1)S(1)} %collective-permute-done.4.refs_2_), channel_id=1, source_target_pairs={{0,56},{8,0},{16,8},{24,16},{32,24},{40,32},{48,40},{56,48},{64,12... | collective-permute-start | bytes 786440 | tf_op jit(solution)/shard_map/ppermute | solution.py:46
  23.0 6.4 %collective-permute-start.5 = (bf16[8,128,128]{2,1,0:T(8,128)(2,1)S(1)}, bf16[8,128,128]{2,1,0:T(8,128)(2,1)S(1)}, u32[]{:S(2)}, u32[]{:S(2)}) collective-permute-start(bf16[8,128,128]{2,1,0:T(8,128)(2,1)S(1)} %collective-permute-done.3.refs_1_), channel_id=1, source_target_pairs={{0,8},{8,16},{16,24},{24,32},{32,40},{40,48},{48,56},{56,0},{64,72... | collective-permute-start | bytes 786440 | tf_op jit(solution)/shard_map/ppermute | solution.py:46
  26.3 6.6 %collective-permute-start.8 = (bf16[8,128,128]{2,1,0:T(8,128)(2,1)S(1)}, bf16[8,128,128]{2,1,0:T(8,128)(2,1)S(1)}, u32[]{:S(2)}, u32[]{:S(2)}) collective-permute-start(bf16[8,128,128]{2,1,0:T(8,128)(2,1)S(1)} %collective-permute-done.6.refs_4_), channel_id=1, source_target_pairs={{0,56},{8,0},{16,8},{24,16},{32,24},{40,32},{48,40},{56,48},{64,12... | collective-permute-start | bytes 786440 | tf_op jit(solution)/shard_map/ppermute | solution.py:46
  29.4 6.8 %collective-permute-start.7 = (bf16[8,128,128]{2,1,0:T(8,128)(2,1)S(1)}, bf16[8,128,128]{2,1,0:T(8,128)(2,1)S(1)}, u32[]{:S(2)}, u32[]{:S(2)}) collective-permute-start(bf16[8,128,128]{2,1,0:T(8,128)(2,1)S(1)} %collective-permute-done.5.refs_3_), channel_id=1, source_target_pairs={{0,8},{8,16},{16,24},{24,32},{32,40},{40,48},{48,56},{56,0},{64,72... | collective-permute-start | bytes 786440 | tf_op jit(solution)/shard_map/ppermute | solution.py:46
  32.9 6.2 %collective-permute-start.10 = (bf16[4,128,128]{2,1,0:T(8,128)(2,1)S(1)}, bf16[4,128,128]{2,1,0:T(8,128)(2,1)S(1)}, u32[]{:S(2)}, u32[]{:S(2)}) collective-permute-start(bf16[4,128,128]{2,1,0:T(8,128)(2,1)S(1)} %slice.25), channel_id=1, source_target_pairs={{0,56},{8,0},{16,8},{24,16},{32,24},{40,32},{48,40},{56,48},{64,12... | collective-permute-start | bytes 393224 | tf_op jit(solution)/shard_map/ppermute | solution.py:46
  36.3 6.5 %collective-permute-start.9 = (bf16[4,128,128]{2,1,0:T(8,128)(2,1)S(1)}, bf16[4,128,128]{2,1,0:T(8,128)(2,1)S(1)}, u32[]{:S(2)}, u32[]{:S(2)}) collective-permute-start(bf16[4,128,128]{2,1,0:T(8,128)(2,1)S(1)} %slice.24), channel_id=1, source_target_pairs={{0,8},{8,16},{16,24},{24,32},{32,40},{40,48},{48,56},{56,0},{64,72... | collective-permute-start | bytes 393224 | tf_op jit(solution)/shard_map/ppermute | solution.py:46
  46.0 8.5 %collective-permute-start.11 = (f32[1056,128]{1,0:T(8,128)S(1)}, f32[1056,128]{1,0:T(8,128)S(1)}, u32[]{:S(2)}, u32[]{:S(2)}) collective-permute-start(f32[1056,128]{1,0:T(8,128)S(1)} %get-tuple-element.33), channel_id=1, source_target_pairs={{0,1},{1,0},{2,3},{3,2},{4,5},{5,4},{6,7},{7,6},{8,9},{9,8},{10,11... | collective-permute-start | bytes 1622024 | tf_op jit(solution)/shard_map/ppermute | solution.py:85
  54.6 6.1 %collective-permute-start.12 = (f32[264,128]{1,0:T(8,128)S(1)}, f32[264,128]{1,0:T(8,128)S(1)}, u32[]{:S(2)}, u32[]{:S(2)}) collective-permute-start(f32[264,128]{1,0:T(8,128)S(1)} %get-tuple-element.35), channel_id=1, source_target_pairs={{0,2},{1,3},{2,4},{3,5},{4,6},{5,7},{6,0},{7,1},{8,10},{9,11},{10,... | collective-permute-start | bytes 405512 | tf_op jit(solution)/shard_map/ppermute | solution.py:89
  55.9 8.7 %collective-permute-start.13 = (f32[264,128]{1,0:T(8,128)S(1)}, f32[264,128]{1,0:T(8,128)S(1)}, u32[]{:S(2)}, u32[]{:S(2)}) collective-permute-start(f32[264,128]{1,0:T(8,128)S(1)} %get-tuple-element.36), channel_id=1, source_target_pairs={{0,4},{1,5},{2,6},{3,7},{4,0},{5,1},{6,2},{7,3},{8,12},{9,13},{10,... | collective-permute-start | bytes 405512 | tf_op jit(solution)/shard_map/ppermute | solution.py:89
  58.4 6.2 %collective-permute-start.14 = (f32[264,128]{1,0:T(8,128)S(1)}, f32[264,128]{1,0:T(8,128)S(1)}, u32[]{:S(2)}, u32[]{:S(2)}) collective-permute-start(f32[264,128]{1,0:T(8,128)S(1)} %get-tuple-element.37), channel_id=1, source_target_pairs={{0,6},{1,7},{2,0},{3,1},{4,2},{5,3},{6,4},{7,5},{8,14},{9,15},{10,... | collective-permute-start | bytes 405512 | tf_op jit(solution)/shard_map/ppermute | solution.py:89
  64.7 6.8 %collective-permute-start.17 = (bf16[2,128,128]{2,1,0:T(8,128)(2,1)S(1)}, bf16[2,128,128]{2,1,0:T(8,128)(2,1)S(1)}, u32[]{:S(2)}, u32[]{:S(2)}) collective-permute-start(bf16[2,128,128]{2,1,0:T(8,128)(2,1)S(1)} %get-tuple-element.38), channel_id=1, source_target_pairs={{0,128},{64,192},{128,0},{192,64},{8,136},{72,200},{136,8},{200,72... | collective-permute-start | bytes 196616 | tf_op jit(solution)/shard_map/ppermute | solution.py:46
  64.8 6.7 %collective-permute-start.16 = (bf16[2,128,128]{2,1,0:T(8,128)(2,1)S(1)}, bf16[2,128,128]{2,1,0:T(8,128)(2,1)S(1)}, u32[]{:S(2)}, u32[]{:S(2)}) collective-permute-start(bf16[2,128,128]{2,1,0:T(8,128)(2,1)S(1)} %get-tuple-element.38), channel_id=1, source_target_pairs={{0,192},{64,0},{128,64},{192,128},{8,200},{72,8},{136,72},{200,136... | collective-permute-start | bytes 196616 | tf_op jit(solution)/shard_map/ppermute | solution.py:46
  66.5 5.0 %collective-permute-start.15 = (bf16[2,128,128]{2,1,0:T(8,128)(2,1)S(1)}, bf16[2,128,128]{2,1,0:T(8,128)(2,1)S(1)}, u32[]{:S(2)}, u32[]{:S(2)}) collective-permute-start(bf16[2,128,128]{2,1,0:T(8,128)(2,1)S(1)} %get-tuple-element.38), channel_id=1, source_target_pairs={{0,64},{64,128},{128,192},{192,0},{8,72},{72,136},{136,200},{200,8... | collective-permute-start | bytes 196616 | tf_op jit(solution)/shard_map/ppermute | solution.py:46
  71.6 5.7 %collective-permute-start.19 = (bf16[8,128,128]{2,1,0:T(8,128)(2,1)S(1)}, bf16[8,128,128]{2,1,0:T(8,128)(2,1)S(1)}, u32[]{:S(2)}, u32[]{:S(2)}) collective-permute-start(bf16[8,128,128]{2,1,0:T(8,128)(2,1)S(1)} %constant_dynamic-update-slice_fusion.2.refs_9_), channel_id=1, source_target_pairs={{0,56},{8,0},{16,8},{24,16},{32,24},{40,32},{48,40},{56,48},{64,12... | collective-permute-start | bytes 786440 | tf_op jit(solution)/shard_map/ppermute | solution.py:46
  71.7 7.1 %collective-permute-start.18 = (bf16[8,128,128]{2,1,0:T(8,128)(2,1)S(1)}, bf16[8,128,128]{2,1,0:T(8,128)(2,1)S(1)}, u32[]{:S(2)}, u32[]{:S(2)}) collective-permute-start(bf16[8,128,128]{2,1,0:T(8,128)(2,1)S(1)} %constant_dynamic-update-slice_fusion.2.refs_9_), channel_id=1, source_target_pairs={{0,8},{8,16},{16,24},{24,32},{32,40},{40,48},{48,56},{56,0},{64,72... | collective-permute-start | bytes 786440 | tf_op jit(solution)/shard_map/ppermute | solution.py:46
  77.3 5.2 %collective-permute-start.21 = (bf16[8,128,128]{2,1,0:T(8,128)(2,1)S(1)}, bf16[8,128,128]{2,1,0:T(8,128)(2,1)S(1)}, u32[]{:S(2)}, u32[]{:S(2)}) collective-permute-start(bf16[8,128,128]{2,1,0:T(8,128)(2,1)S(1)} %collective-permute-done.19.refs_11_), channel_id=1, source_target_pairs={{0,56},{8,0},{16,8},{24,16},{32,24},{40,32},{48,40},{56,48},{64,12... | collective-permute-start | bytes 786440 | tf_op jit(solution)/shard_map/ppermute | solution.py:46
  78.8 6.4 %collective-permute-start.20 = (bf16[8,128,128]{2,1,0:T(8,128)(2,1)S(1)}, bf16[8,128,128]{2,1,0:T(8,128)(2,1)S(1)}, u32[]{:S(2)}, u32[]{:S(2)}) collective-permute-start(bf16[8,128,128]{2,1,0:T(8,128)(2,1)S(1)} %collective-permute-done.18.refs_10_), channel_id=1, source_target_pairs={{0,8},{8,16},{16,24},{24,32},{32,40},{40,48},{48,56},{56,0},{64,72... | collective-permute-start | bytes 786440 | tf_op jit(solution)/shard_map/ppermute | solution.py:46
  82.5 6.6 %collective-permute-start.23 = (bf16[8,128,128]{2,1,0:T(8,128)(2,1)S(1)}, bf16[8,128,128]{2,1,0:T(8,128)(2,1)S(1)}, u32[]{:S(2)}, u32[]{:S(2)}) collective-permute-start(bf16[8,128,128]{2,1,0:T(8,128)(2,1)S(1)} %collective-permute-done.21.refs_13_), channel_id=1, source_target_pairs={{0,56},{8,0},{16,8},{24,16},{32,24},{40,32},{48,40},{56,48},{64,12... | collective-permute-start | bytes 786440 | tf_op jit(solution)/shard_map/ppermute | solution.py:46
  85.2 6.5 %collective-permute-start.22 = (bf16[8,128,128]{2,1,0:T(8,128)(2,1)S(1)}, bf16[8,128,128]{2,1,0:T(8,128)(2,1)S(1)}, u32[]{:S(2)}, u32[]{:S(2)}) collective-permute-start(bf16[8,128,128]{2,1,0:T(8,128)(2,1)S(1)} %collective-permute-done.20.refs_12_), channel_id=1, source_target_pairs={{0,8},{8,16},{16,24},{24,32},{32,40},{40,48},{48,56},{56,0},{64,72... | collective-permute-start | bytes 786440 | tf_op jit(solution)/shard_map/ppermute | solution.py:46
  89.1 12.4 %collective-permute-start.25 = (bf16[4,128,128]{2,1,0:T(8,128)(2,1)S(1)}, bf16[4,128,128]{2,1,0:T(8,128)(2,1)S(1)}, u32[]{:S(2)}, u32[]{:S(2)}) collective-permute-start(bf16[4,128,128]{2,1,0:T(8,128)(2,1)S(1)} %slice.27), channel_id=1, source_target_pairs={{0,56},{8,0},{16,8},{24,16},{32,24},{40,32},{48,40},{56,48},{64,12... | collective-permute-start | bytes 393224 | tf_op jit(solution)/shard_map/ppermute | solution.py:46
  91.7 14.7 %collective-permute-start.24 = (bf16[4,128,128]{2,1,0:T(8,128)(2,1)S(1)}, bf16[4,128,128]{2,1,0:T(8,128)(2,1)S(1)}, u32[]{:S(2)}, u32[]{:S(2)}) collective-permute-start(bf16[4,128,128]{2,1,0:T(8,128)(2,1)S(1)} %slice.26), channel_id=1, source_target_pairs={{0,8},{8,16},{16,24},{24,32},{32,40},{40,48},{48,56},{56,0},{64,72... | collective-permute-start | bytes 393224 | tf_op jit(solution)/shard_map/ppermute | solution.py:46
  114.5 8.6 %collective-permute-start.26 = (bf16[8,176,128]{2,1,0:T(8,128)(2,1)S(1)}, bf16[8,176,128]{2,1,0:T(8,128)(2,1)S(1)}, u32[]{:S(2)}, u32[]{:S(2)}) collective-permute-start(bf16[8,176,128]{2,1,0:T(8,128)(2,1)S(1)} %get-tuple-element.40), channel_id=1, source_target_pairs={{0,1},{1,0},{2,3},{3,2},{4,5},{5,4},{6,7},{7,6},{8,9},{9,8},{10,11... | collective-permute-start | bytes 1081352 | tf_op jit(solution)/shard_map/ppermute | solution.py:85
  123.2 5.1 %collective-permute-start.27 = (bf16[2,176,128]{2,1,0:T(8,128)(2,1)S(1)}, bf16[2,176,128]{2,1,0:T(8,128)(2,1)S(1)}, u32[]{:S(2)}, u32[]{:S(2)}) collective-permute-start(bf16[2,176,128]{2,1,0:T(8,128)(2,1)S(1)} %get-tuple-element.42), channel_id=1, source_target_pairs={{0,2},{1,3},{2,4},{3,5},{4,6},{5,7},{6,0},{7,1},{8,10},{9,11},{10,... | collective-permute-start | bytes 270344 | tf_op jit(solution)/shard_map/ppermute | solution.py:89
  124.4 6.4 %collective-permute-start.28 = (bf16[2,176,128]{2,1,0:T(8,128)(2,1)S(1)}, bf16[2,176,128]{2,1,0:T(8,128)(2,1)S(1)}, u32[]{:S(2)}, u32[]{:S(2)}) collective-permute-start(bf16[2,176,128]{2,1,0:T(8,128)(2,1)S(1)} %get-tuple-element.43), channel_id=1, source_target_pairs={{0,4},{1,5},{2,6},{3,7},{4,0},{5,1},{6,2},{7,3},{8,12},{9,13},{10,... | collective-permute-start | bytes 270344 | tf_op jit(solution)/shard_map/ppermute | solution.py:89
  126.5 4.6 %collective-permute-start.29 = (bf16[2,176,128]{2,1,0:T(8,128)(2,1)S(1)}, bf16[2,176,128]{2,1,0:T(8,128)(2,1)S(1)}, u32[]{:S(2)}, u32[]{:S(2)}) collective-permute-start(bf16[2,176,128]{2,1,0:T(8,128)(2,1)S(1)} %get-tuple-element.44), channel_id=1, source_target_pairs={{0,6},{1,7},{2,0},{3,1},{4,2},{5,3},{6,4},{7,5},{8,14},{9,15},{10,... | collective-permute-start | bytes 270344 | tf_op jit(solution)/shard_map/ppermute | solution.py:89
  134.1 7.4 %collective-permute-start.33 = (bf16[4,176,128]{2,1,0:T(8,128)(2,1)S(1)}, bf16[4,176,128]{2,1,0:T(8,128)(2,1)S(1)}, u32[]{:S(2)}, u32[]{:S(2)}) collective-permute-start(bf16[4,176,128]{2,1,0:T(8,128)(2,1)S(1)} %constant_dynamic-update-slice_fusion.6.w0), channel_id=1, source_target_pairs={{0,4},{1,5},{2,6},{3,7},{4,0},{5,1},{6,2},{7,3},{8,12},{9,13},{10,... | collective-permute-start | bytes 540680 | tf_op jit(solution)/shard_map/ppermute | solution.py:89
  136.9 8.8 %collective-permute-start.32 = (bf16[4,176,128]{2,1,0:T(8,128)(2,1)S(1)}, bf16[4,176,128]{2,1,0:T(8,128)(2,1)S(1)}, u32[]{:S(2)}, u32[]{:S(2)}) collective-permute-start(bf16[4,176,128]{2,1,0:T(8,128)(2,1)S(1)} %constant_dynamic-update-slice_fusion.6.w0), channel_id=1, source_target_pairs={{0,6},{1,7},{2,0},{3,1},{4,2},{5,3},{6,4},{7,5},{8,14},{9,15},{10,... | collective-permute-start | bytes 540680 | tf_op jit(solution)/shard_map/ppermute | solution.py:89
  137.9 7.9 %collective-permute-start.31 = (bf16[4,176,128]{2,1,0:T(8,128)(2,1)S(1)}, bf16[4,176,128]{2,1,0:T(8,128)(2,1)S(1)}, u32[]{:S(2)}, u32[]{:S(2)}) collective-permute-start(bf16[4,176,128]{2,1,0:T(8,128)(2,1)S(1)} %constant_dynamic-update-slice_fusion.6.w0), channel_id=1, source_target_pairs={{0,2},{1,3},{2,4},{3,5},{4,6},{5,7},{6,0},{7,1},{8,10},{9,11},{10,... | collective-permute-start | bytes 540680 | tf_op jit(solution)/shard_map/ppermute | solution.py:89
  (13 other events, 357.1 us)
